TPU v7x, 32 devices: a whole 2x2x4 slice. The times are simulated.
32 devices in a mesh: src: 8 (over z, y), tgt: 4 (over x, core).
Axes of the slice: x: 2, y: 2, z: 4, core: 2. Of those that a mesh axis runs over, the one named last changes fastest.
Arguments:
- coefficients: float32 [256, 128, 512], P(('src', 'tgt')), may hold values from -6 to 6
- transfer: float32 [8, 256, 128, 256], P(None, ('src', 'tgt')), may hold values from -0.375 to 0.375
- local_bits: int32 [4], replicated, may hold values from 0 to 2
- relabel: int32 [1024], replicated, may hold values from 0 to 1023, each once
Outputs:
- result: float32 [256, 128, 512], P(('src', 'tgt'))
Inputs may be any that keep to these rules, and one draw needn't show every extreme that they name: `local_bits`: each entry names a bit of a node's position among the 8 nodes of one device. `relabel`: a permutation of the 1024 rows of one device.
All inputs are finite; a program needn't handle non-finite values.
Results may differ from a plain program's by a relative error of at most 0.00007.
Values sent between devices are 32-bit elements; how exact they have to be, the bound alone decides.
No kernel may reach another device: no remote copies, remote signals or barrier semaphores. Data moves between devices by JAX's collectives and lax.ppermute only.
A program may use at most 64 MiB of HBM per device.

v0:
```python
import functools

import jax
import jax.numpy as jnp
from jax import lax
from jax.experimental import pallas as pl
from jax.experimental.pallas import tpu as pltpu
from jax.sharding import PartitionSpec as P

F32, BF16 = jnp.float32, jnp.bfloat16
GROUP = 128
CUTS = (1, 1, 1, 1)
PAD = 8
PAD_X = 8
WINDOW = 2
CORE_SPLIT = 2
Y_CUTS = (2, 2, 2, 2)
JOINT = 0
STAGES = (1, 3, 4, 6)
VMEM_LIMIT = 16 * 1024 * 1024
FIRST_LIMIT = 62 * 1024 * 1024


def partner_2(shard, axis, mask):
    return lax.ppermute(shard, axis, [(i, i ^ mask) for i in range(lax.axis_size(axis))])


def split2(x):
    high = x.astype(BF16)
    return high, (x - high.astype(F32)).astype(BF16)


def split3(x):
    high = x.astype(BF16)
    rest = x - high.astype(F32)
    middle = rest.astype(BF16)
    return high, middle, (rest - middle.astype(F32)).astype(BF16)


def product(blocks, x):
    half, width = blocks.shape[0] // 2, x.shape[1]
    out = jnp.dot(blocks, jnp.concatenate(split2(x), axis=1), preferred_element_type=F32)
    return (out[:half, :width] + out[:half, width:]) + (out[half:, :width] + out[half:, width:])


def unpack(refs, first, count, parts, extra=0):
    each = refs[0].shape[0] - extra
    width = refs[0].shape[1] // parts
    run = each * len(refs)
    lane = first // run * width
    place = first % run
    return refs[place // each][place % each:place % each + count, lane:lane + width]


def pack(out_ref, rows, parts):
    run = out_ref.shape[0]
    out_ref[...] = jnp.concatenate([rows[part * run:(part + 1) * run, :] for part in range(parts)], axis=1)


def local_level(state, rank, blocks, bit, put, lanes=slice(None)):
    nodes = state.shape[0] // rank
    for index in range(nodes // 2):
        low_bits = jnp.bitwise_and(index, jnp.left_shift(1, bit) - 1)
        low = jnp.left_shift(jnp.right_shift(index, bit), bit + 1) | low_bits
        high = low | jnp.left_shift(1, bit)
        spans = [pl.ds(pl.multiple_of(node * rank, rank), rank) for node in (low, high)]
        both = jnp.concatenate([state[span, lanes] for span in spans], axis=0)
        out = product(blocks(low, high), both)
        put(spans[0], out[:rank])
        put(spans[1], out[rank:])


def split_blocks(ref, level):
    rank = ref.shape[2] // 2

    def blocks(low, high):
        return jnp.concatenate(
            [ref[level, low, :rank], ref[level, high, :rank], ref[level, low, rank:], ref[level, high, rank:]],
            axis=0,
        )

    return blocks


def packed_level(state, blocks, level, bit, outs, after, parts):
    rank = blocks.shape[2] // 2
    target = outs[0] if parts == 1 and len(outs) == 1 else after

    def put(span, value):
        target[span, :] = value

    local_level(state, rank, split_blocks(blocks, level), bit, put)
    if target is after:
        each = outs[0].shape[0]
        run = each * len(outs)
        for index, out_ref in enumerate(outs):
            row = [after[part * run + index * each:part * run + (index + 1) * each] for part in range(parts)]
            out_ref[...] = row[0] if parts == 1 else jnp.concatenate(row, axis=1)


def first_kernel(chunks, bits, x_hbm, g_hbm, *rest):
    outs, (x_ref, g_ref, after, arrived) = rest[-4 - len(chunks):-4], rest[-4:]
    nodes, rank, _ = x_ref.shape
    lanes = outs[0].shape[1]
    first, groups = chunks[0][0], x_ref.shape[2] // lanes
    x_copy = pltpu.make_async_copy(
        x_hbm.at[:, :, first * lanes:(first + groups) * lanes], x_ref, arrived.at[0]
    )
    g_copy = pltpu.make_async_copy(g_hbm.at[0], g_ref, arrived.at[1])
    x_copy.start()
    g_copy.start()
    x_copy.wait()
    g_copy.wait()
    state = x_ref.reshape(nodes * rank, x_ref.shape[2])

    def blocks(low, high):
        top = jnp.concatenate([g_ref[low], g_ref[high]], axis=0)
        return jnp.concatenate(split2(top), axis=0)

    for (group, part, parts), out_ref in zip(chunks, outs):
        width = lanes // parts
        begin = (group - first) * lanes + part * width
        run = out_ref.shape[0] - PAD

        def put(span, value):
            if parts == 1:
                out_ref[span, :] = value
            else:
                after[span, :width] = value

        local_level(state, rank, blocks, bits[0], put, slice(begin, begin + width))
        if parts > 1:
            out_ref[:run, :] = jnp.concatenate(
                [after[at * run:(at + 1) * run, :width] for at in range(parts)], axis=1
            )
        out_ref[run:, :] = jnp.zeros((PAD, lanes), F32)


def release_kernel(*_):
    pass


def prepare_kernel(g_hbm, *rest):
    outs, (g_ref, arrived) = rest[-2 - len(STAGES):-2], rest[-2:]
    levels, nodes, rank, _ = g_ref.shape
    copies = [
        pltpu.make_async_copy(g_hbm.at[level + 1], g_ref.at[level], arrived.at[level])
        for level in range(levels)
    ]
    for copy in copies:
        copy.start()
    for first, out_ref in zip(STAGES, outs):
        for offset in range(out_ref.shape[0]):
            level = first - 1 + offset
            copies[level].wait()

            def split(node, carry):
                high, low = split2(g_ref[level, node])
                out_ref[offset, node, :rank] = high
                out_ref[offset, node, rank:] = low
                return carry

            lax.fori_loop(0, nodes, split, 0)


def choose_kernel(axis, relabel_ref, *rest):
    out_ref = rest[-1]
    rows = out_ref.shape[0]
    count = lax.axis_size(axis)
    half, piece_rows = count // 2, rows // count
    group = lax.axis_index(axis) % half
    for offset in range(half):
        for side in range(2):
            piece = side * half + jnp.bitwise_xor(group, offset)
            start = pl.multiple_of(piece * piece_rows, piece_rows)
            wanted = relabel_ref[pl.ds(start, piece_rows), :]
            column = lax.broadcasted_iota(jnp.int32, (piece_rows, rows), 1)
            place = (offset * 2 + side) * piece_rows
            out_ref[place:place + piece_rows, :] = jnp.where(wanted == column, 1.0, 0.0).astype(BF16)


def cross_level(put, axis, shift, blocks, level, take_own, take_other):
    upper = jnp.bitwise_and(jnp.right_shift(lax.axis_index(axis), shift), 1) == 1
    nodes, rank = blocks.shape[1], blocks.shape[2] // 2
    for node in range(nodes):
        own, other = take_own(node * rank, rank), take_other(node * rank, rank)
        leading = jnp.where(upper, other, own)
        trailing = jnp.where(upper, own, other)
        value = product(blocks[level, node], jnp.concatenate([leading, trailing], axis=0))
        put(node * rank, rank, value)


def put_rows(ref):
    def put(first, count, value):
        ref[first:first + count, :] = value

    return put


def pair_kernel(parts, cuts, axis, shift, level, slot, bits, blocks, own, other, *rest):
    outs, before, after = rest[-2 - cuts:-2], *rest[-2:]
    cross_level(
        put_rows(before), axis, shift, blocks, level,
        lambda first, count: unpack([own], first, count, parts, PAD),
        lambda first, count: unpack([other], first, count, parts, PAD),
    )
    packed_level(before, blocks, level + 1, bits[slot], outs, after, parts)


def last_kernel(parts, part, done, axis, shift, level, slot, bits, blocks, *rest):
    own, other, rest = rest[:CORE_SPLIT], rest[CORE_SPLIT:2 * CORE_SPLIT], rest[2 * CORE_SPLIT:]
    out_ref, before, after, sent = rest[-4:]
    nodes, rank = blocks.shape[1], blocks.shape[2] // 2
    width = before.shape[1]
    lanes = after.shape[1]
    earlier = rest[:1] if part else ()
    copies = [
        pltpu.make_async_copy(
            ref.reshape(nodes, rank, lanes), out_ref.at[:, :, at * lanes:(at + 1) * lanes], sent.at[at]
        )
        for at, ref in enumerate([*rest[len(earlier):len(earlier) + done], after] if done else [])
    ]
    for copy in copies[:-1]:
        copy.start()
    cross_level(
        put_rows(before), axis, shift, blocks, level,
        lambda first, count: unpack(own, first, count, parts),
        lambda first, count: unpack(other, first, count, parts),
    )
    target = after if done else out_ref
    for ref in earlier:
        target[...] = ref[...]

    def put(span, value):
        target[span, part * width:(part + 1) * width] = value

    local_level(before, rank, split_blocks(blocks, level + 1), bits[slot], put)
    for copy in copies[-1:]:
        copy.start()
    for copy in copies:
        copy.wait()


def relabel_kernel(parts, cuts, count, joint, axis, shift, level, blocks, chosen, *rest):
    own, other = rest[:cuts], rest[cuts:2 * cuts]
    spread = rest[-1]
    outs = [[rest[-3].at[offset]] for offset in range(count)] if joint else [[ref] for ref in rest[-1 - count:-1]]
    if joint:
        outs[1 % count].append(rest[-2])
    width = spread.shape[1] // 3

    def put(first, size, value):
        spread[first:first + size] = jnp.concatenate(split3(value), axis=1)

    cross_level(
        put, axis, shift, blocks, level,
        lambda first, size: unpack(own, first, size, parts),
        lambda first, size: unpack(other, first, size, parts),
    )
    piece_rows = spread.shape[0] // (2 * count)
    for index, targets in enumerate(outs):
        for side in range(2):
            place = (index * 2 + side) * piece_rows
            out = jnp.dot(chosen[place:place + piece_rows], spread[...], preferred_element_type=F32)
            out = (out[:, :width] + out[:, width:2 * width]) + out[:, 2 * width:]
            for target in targets:
                pack(target.at[side, :piece_rows // parts], out, parts)


def gather_kernel(parts, count, picks, axis, level, slot, bits, blocks, *rest):
    received, outs = rest[:count], rest[-3 - CORE_SPLIT:-3]
    both, before, after = rest[-3:]
    me = lax.axis_index(axis)
    rows, width = both.shape[1:]
    piece_rows = rows // count
    run = piece_rows // parts
    for offset, ref in enumerate(received):
        ref = ref if picks[offset] is None else ref.at[picks[offset]]
        start = pl.multiple_of(jnp.bitwise_xor(me, offset) * piece_rows, piece_rows)
        for side in range(2):
            for part in range(parts):
                both[side, pl.ds(start + part * run, run), :] = ref[
                    side, :run, part * width:(part + 1) * width
                ]
    nodes, rank = blocks.shape[1], blocks.shape[2] // 2
    for node in range(nodes):
        span = slice(node * rank, (node + 1) * rank)
        before[span] = product(
            blocks[level, node], jnp.concatenate([both[0, span], both[1, span]], axis=0)
        )
    packed_level(before, blocks, level + 1, bits[slot], outs, after, parts)


SMEM = pl.BlockSpec(memory_space=pltpu.SMEM)
VMEM = pl.BlockSpec(memory_space=pltpu.VMEM)
HBM = pl.BlockSpec(memory_space=pltpu.HBM)
ANY = pl.BlockSpec(memory_space=pl.ANY)


def on_device(coefficients, transfer, local_bits, relabel):
    levels = transfer.shape[0]
    nodes, rank, columns = coefficients.shape
    rows = nodes * rank
    n_src, n_tgt = lax.axis_size("src"), lax.axis_size("tgt")
    src_far, tgt_far = n_src // 2, n_tgt // 2
    shape = jax.ShapeDtypeStruct
    chunks = [(group, part, parts) for group, parts in enumerate(CUTS) for part in range(parts)]
    store = {}

    def run(kernel, out_shape, in_specs, out_specs, scratch, args, aliases=None, limit=VMEM_LIMIT):
        extra = [store["token"]] if "token" in store else []
        out = pl.pallas_call(
            kernel,
            out_shape=out_shape,
            in_specs=list(in_specs) + [ANY] * len(extra),
            out_specs=out_specs,
            scratch_shapes=scratch,
            input_output_aliases=aliases or {},
            compiler_params=pltpu.CompilerParams(vmem_limit_bytes=limit),
            cost_estimate=pl.CostEstimate(flops=0, bytes_accessed=0, transcendentals=0),
        )(*args, *extra)
        store["token"] = out[0]
        return out

    def packed(parts, count=1):
        return [shape((rows // parts // count, GROUP), F32)] * count

    def narrow(parts, count):
        return [pltpu.VMEM((rows, GROUP // parts), F32)] * count

    def step_a(index):
        wanted = chunks[1:] if index else chunks[:1]
        groups = wanted[-1][0] - wanted[0][0] + 1
        out = run(
            functools.partial(first_kernel, tuple(wanted)),
            [shape((rows // parts + PAD, GROUP), F32) for _, _, parts in wanted],
            [SMEM, HBM, HBM],
            [VMEM] * len(wanted),
            [
                pltpu.VMEM((nodes, rank, groups * GROUP), F32),
                pltpu.VMEM(transfer.shape[1:], F32),
                pltpu.VMEM((rows, GROUP), F32),
                pltpu.SemaphoreType.DMA((2,)),
            ],
            [local_bits, coefficients, transfer],
            limit=FIRST_LIMIT,
        )
        for offset, array in enumerate(out):
            store["whole", index + offset] = array
        if index < WINDOW:
            store["far", index] = partner_2(out[0], "src", src_far)

    def step_p(_):
        ends = STAGES[1:] + (levels,)
        blocks = run(
            prepare_kernel,
            [shape((end - first, nodes, 2 * rank, 2 * rank), BF16) for first, end in zip(STAGES, ends)],
            [HBM],
            [VMEM] * len(STAGES),
            [pltpu.VMEM((levels - 1,) + transfer.shape[1:], F32), pltpu.SemaphoreType.DMA((levels - 1,))],
            [transfer],
        )
        for first, array in zip(STAGES, blocks):
            store["blocks", first] = array

    def step_q(_):
        store["chosen"] = run(
            functools.partial(choose_kernel, "tgt"),
            [shape((rows, rows), BF16)],
            [VMEM],
            [VMEM],
            [],
            [relabel.reshape(rows, 1)],
        )[0]

    def step_r(index):
        array = store["whole", index]
        array = run(
            release_kernel,
            [shape(array.shape, F32)],
            [ANY, ANY],
            [ANY],
            [],
            [array, store["far", index - WINDOW]],
            aliases={0: 0},
        )[0]
        store["whole", index] = array
        store["far", index] = partner_2(array, "src", src_far)

    def step_b(index):
        _, _, parts = chunks[index]
        cuts = Y_CUTS[index]
        ended = []
        own = run(
            functools.partial(pair_kernel, parts, cuts, "src", src_far.bit_length() - 1, 0, 1),
            packed(parts, cuts),
            [SMEM, VMEM, VMEM, VMEM] + [ANY] * len(ended),
            [VMEM] * cuts,
            narrow(parts, 2),
            [local_bits, store["blocks", 1], store["whole", index], store["far", index], *ended],
        )
        store["own", index] = own
        store["near", index] = [partner_2(piece, "src", 1) for piece in own]

    def step_c(index):
        _, _, parts = chunks[index]
        cuts = Y_CUTS[index]
        joint = index < JOINT
        piece = (2, rows // n_tgt // parts, GROUP)
        pieces = run(
            functools.partial(relabel_kernel, parts, cuts, tgt_far, joint, "src", 0, 0),
            [shape((tgt_far, 2, piece[1] + PAD_X, GROUP), F32), shape(piece, F32)] if joint else [shape(piece, F32)] * tgt_far,
            [VMEM] * (2 + 2 * cuts),
            [VMEM] * (2 if joint else tgt_far),
            [pltpu.VMEM((rows, 3 * GROUP // parts), BF16)],
            [store["blocks", 3], store["chosen"], *store["own", index], *store["near", index]],
        )
        for offset, piece in enumerate(pieces):
            store["piece", index, offset] = piece

    def step_t(index):
        store["moved", index, 1] = partner_2(store["piece", index, 1 % tgt_far], "tgt", 1)

    def step_x(index):
        if index >= JOINT:
            for offset in range(2, n_tgt):
                store["moved", index, offset] = partner_2(
                    store["piece", index, offset % tgt_far], "tgt", offset
                )
            return
        joint = store["piece", index, 0]
        for offset in range(2, n_tgt, 2):
            first = offset % tgt_far
            both = joint if tgt_far == 2 else joint[first:first + 2]
            store["moved", index, offset] = partner_2(both, "tgt", offset)

    def step_s(index):
        if index < JOINT:
            for offset in range(2, n_tgt, 2):
                store["moved", index, offset + 1] = partner_2(store["moved", index, offset][1], "tgt", 1)

    def step_d(index):
        _, _, parts = chunks[index]
        joint = index < JOINT
        picks = tuple(0 if joint and offset % 2 == 0 else None for offset in range(n_tgt))
        store["mid", index] = run(
            functools.partial(gather_kernel, parts, n_tgt, picks, "tgt", 0, 2),
            packed(parts, CORE_SPLIT),
            [SMEM, VMEM] + [VMEM] * n_tgt,
            [VMEM] * CORE_SPLIT,
            [pltpu.VMEM((2, rows, GROUP // parts), F32)] + narrow(parts, 2),
            [
                local_bits, store["blocks", 4], store["piece", index, 0],
                *(store["moved", index, offset] for offset in range(1, n_tgt)),
            ],
        )
        store["core", index] = [partner_2(piece, "tgt", 1) for piece in store["mid", index]]

    def step_e(index):
        group, part, parts = chunks[index]
        final = index == len(chunks) - 1
        earlier = [store["out", index - 1]] if part else []
        if final:
            earlier += [store["out", chunks.index((at, count - 1, count))] for at, count in enumerate(CUTS[:-1])]
        store["out", index] = run(
            functools.partial(last_kernel, parts, part, len(CUTS) - 1 if final else 0, "tgt", 0, 0, 3),
            [shape((nodes, rank, columns) if final else (rows, GROUP), F32)],
            [SMEM, VMEM] + [VMEM] * (2 * CORE_SPLIT + len(earlier)),
            [HBM if final else VMEM],
            narrow(parts, 1) + [pltpu.VMEM((rows, GROUP), F32), pltpu.SemaphoreType.DMA((len(CUTS),))],
            [local_bits, store["blocks", 6], *store["mid", index], *store["core", index], *earlier],
        )[0]

    steps = {
        "A": step_a, "P": step_p, "Q": step_q, "R": step_r,
        "B": step_b, "C": step_c, "T": step_t, "X": step_x, "S": step_s, "D": step_d, "E": step_e,
    }

    def follow(names):
        for name in names:
            steps[name[0]](int(name[1:]))

    kept = ("piece", "moved", "out")

    def apart(names):
        def work():
            before = dict(store)
            follow(names)
            made = {key: value for key, value in store.items() if before.get(key) is not value and key[0] in kept}
            keys.extend(key for key in made if key not in keys)
            store.clear()
            store.update(before)
            return list(made.values())

        keys = []
        shapes = jax.eval_shape(work)
        made = lax.cond(
            local_bits[0] >= 0, work, lambda: jax.tree.map(lambda x: jnp.zeros(x.shape, x.dtype), shapes)
        )
        store.update(zip(keys, made))
        store["token"] = made[0]

    for names in ORDER:
        if isinstance(names, str):
            follow([names])
        else:
            apart(names)
    return store["out", len(chunks) - 1]


ORDER = (
    'A0',
    'A1',
    'P0',
    'Q0',
    'R2',
    'B0',
    'R3',
    'B1',
    'C0',
    'T0',
    'X0',
    'B2',
    'C1',
    'T1',
    'X1',
    'D0',
    'B3',
    'C2',
    'T2',
    'X2',
    'D1',
    'E0',
    'C3',
    'T3',
    'X3',
    'D2',
    'E1',
    'D3',
    'E2',
    'E3',
)


def solution(mesh):
    placed = (P(("src", "tgt"), None, None), P(None, ("src", "tgt"), None, None), P(), P())
    return jax.shard_map(
        on_device,
        mesh=mesh,
        in_specs=placed,
        out_specs=P(("src", "tgt"), None, None),
        check_vma=False,
    )
```

profile of v0, /device:TPU:0, one launch (start us, length us, event | category | flops | bytes accessed | tf_op | source)
XLA Modules:
  0.0 142.3 jit_solution(16944362836847409872)
XLA Ops:
  0.0 3.3 %shard_map.46.rest_0_.own = f32[1032,128]{1,0:T(8,128)} custom-call(s32[4]{0:T(128)} %bits.27, f32[8,128,512]{2,1,0:T(8,128)} %x_hbm.3, f32[8,8,128,256]{3,2,1,0:T(8,128)} %g_hbm.5), custom_call_target="tpu_custom_call" | custom-call | tf_op jit(solution)/shard_map/pallas_call | solution.py:312
  3.3 4.1 %collective-permute-start.1 = (f32[1032,128]{1,0:T(8,128)}, f32[1032,128]{1,0:T(8,128)}, u32[]{:S(2)}, u32[]{:S(2)}) collective-permute-start(f32[1032,128]{1,0:T(8,128)} %shard_map.46.rest_0_.own), channel_id=1, source_target_pairs={{0,16},{4,20},{8,24},{12,28},{16,0},{20,4},{24,8},{28,12},{1,17},{... | collective-permute-start | bytes 1585160 | tf_op jit(solution)/shard_map/ppermute | solution.py:25
  7.4 4.5 %shard_map.47 = (f32[1032,128]{1,0:T(8,128)}, f32[1032,128]{1,0:T(8,128)}, f32[1032,128]{1,0:T(8,128)}) custom-call(s32[4]{0:T(128)} %bits.27, f32[8,128,512]{2,1,0:T(8,128)} %x_hbm.3, f32[8,8,128,256]{3,2,1,0:T(8,128)} %g_hbm.5, f32[1032,128]{1,0:T(8,128)} %shard_map.46.rest_0_.own), custom_call_target="tpu_custom_call" | custom-call | tf_op jit(solution)/shard_map/pallas_call | solution.py:312
  12.1 3.4 %copy-done = f32[8,8,128,256]{3,2,1,0:T(8,128)S(1)} copy-done((f32[8,8,128,256]{3,2,1,0:T(8,128)S(1)}, f32[8,8,128,256]{3,2,1,0:T(8,128)}, u32[]{:S(2)}) %copy-start) | copy-done | bytes 8388632
  15.4 1.0 copy-done.8
  16.5 1.6 %shard_map.48 = (bf16[2,8,256,256]{3,2,1,0:T(8,128)(2,1)S(1)}, bf16[1,8,256,256]{3,2,1,0:T(8,128)(2,1)S(1)}, bf16[2,8,256,256]{3,2,1,0:T(8,128)(2,1)S(1)}, bf16[2,8,256,256]{3,2,1,0:T(8,128)(2,1)S(1)}) custom-call(f32[8,8,128,256]{3,2,1,0:T(8,128)S(1)} %copy-done, f32[1032,128]{1,0:T(8,128)S(1)} %copy-done.8), custom_call_target="tpu_custom_call" | custom-call | tf_op jit(solution)/shard_map/pallas_call | solution.py:312
  18.1 1.3 copy-done.1
  19.4 1.3 copy-done.3
  20.8 1.0 copy.7.relabel_ref
  21.8 1.0 copy-done.10
  23.3 20.0 %collective-permute-done.1.__1_.other = f32[1032,128]{1,0:T(8,128)} collective-permute-done((f32[1032,128]{1,0:T(8,128)}, f32[1032,128]{1,0:T(8,128)}, u32[]{:S(2)}, u32[]{:S(2)}) %collective-permute-start.1) | collective-permute-done | bytes 528416 | tf_op jit(solution)/shard_map/ppermute | solution.py:25
  43.4 2.1 %shard_map.51 = (f32[512,128]{1,0:T(8,128)S(1)}, f32[512,128]{1,0:T(8,128)S(1)}) custom-call(s32[4]{0:T(128)S(1)} %copy-done.11, bf16[2,8,256,256]{3,2,1,0:T(8,128)(2,1)S(1)} %get-tuple-element.40.rest_0_.blocks, f32[1032,128]{1,0:T(8,128)S(1)} %copy-done.5, f32[1032,128]{1,0:T(8,128)} %collective-permute-done.1.__1_.other, ...), custom_call_target="tpu_custom_call" | custom-call | tf_op jit(solution)/shard_map/pallas_call | solution.py:312
  45.4 1.9 %collective-permute-start.3 = (f32[512,128]{1,0:T(8,128)S(1)}, f32[512,128]{1,0:T(8,128)S(1)}, u32[]{:S(2)}, u32[]{:S(2)}) collective-permute-start(f32[512,128]{1,0:T(8,128)S(1)} %get-tuple-element.43.__2_.rest_0_), channel_id=1, source_target_pairs={{0,4},{4,0},{8,12},{12,8},{16,20},{20,16},{24,28},{28,24},{1,5},{5... | collective-permute-start | bytes 786440 | tf_op jit(solution)/shard_map/ppermute | solution.py:25
  47.5 18.4 %collective-permute-done.__1_.other = f32[1032,128]{1,0:T(8,128)} collective-permute-done((f32[1032,128]{1,0:T(8,128)}, f32[1032,128]{1,0:T(8,128)}, u32[]{:S(2)}, u32[]{:S(2)}) %collective-permute-start) | collective-permute-done | bytes 528416 | tf_op jit(solution)/shard_map/ppermute | solution.py:25
  65.9 2.0 %shard_map.53 = (f32[512,128]{1,0:T(8,128)S(1)}, f32[512,128]{1,0:T(8,128)S(1)}) custom-call(s32[4]{0:T(128)S(1)} %copy-done.11, bf16[2,8,256,256]{3,2,1,0:T(8,128)(2,1)S(1)} %get-tuple-element.40.rest_0_.blocks, f32[1032,128]{1,0:T(8,128)S(1)} %copy-done.9, f32[1032,128]{1,0:T(8,128)} %collective-permute-done.__1_.other, f32[1032,128]{1,0:T(8,128)S(1)} %shard_map.52.rest_0_.own), custom_call_target="tpu_custom_call" | custom-call | tf_op jit(solution)/shard_map/pallas_call | solution.py:312
  67.9 1.9 %collective-permute-start.8 = (f32[512,128]{1,0:T(8,128)S(1)}, f32[512,128]{1,0:T(8,128)S(1)}, u32[]{:S(2)}, u32[]{:S(2)}) collective-permute-start(f32[512,128]{1,0:T(8,128)S(1)} %get-tuple-element.45.rest_4_.rest_0_), channel_id=1, source_target_pairs={{0,4},{4,0},{8,12},{12,8},{16,20},{20,16},{24,28},{28,24},{1,5},{5... | collective-permute-start | bytes 786440 | tf_op jit(solution)/shard_map/ppermute | solution.py:25
  70.0 1.6 %shard_map.54 = (f32[2,256,128]{2,1,0:T(8,128)S(1)}, f32[2,256,128]{2,1,0:T(8,128)S(1)}) custom-call(bf16[1,8,256,256]{3,2,1,0:T(8,128)(2,1)S(1)} %get-tuple-element.39.blocks, bf16[1024,1024]{1,0:T(8,128)(2,1)S(1)} %shard_map.49.__2_.chosen, f32[512,128]{1,0:T(8,128)S(1)} %get-tuple-element.43.__2_.rest_0_, f32[512,128]{1,0:T(8,128)S(1)} %get-tuple-element.44.rest_1_, ...), custom_call_target="tpu_custom_call" | custom-call | tf_op jit(solution)/shard_map/pallas_call | solution.py:312
  71.7 5.6 %collective-permute-done.8.rest_2_ = f32[512,128]{1,0:T(8,128)S(1)} collective-permute-done((f32[512,128]{1,0:T(8,128)S(1)}, f32[512,128]{1,0:T(8,128)S(1)}, u32[]{:S(2)}, u32[]{:S(2)}) %collective-permute-start.8) | collective-permute-done | bytes 262176 | tf_op jit(solution)/shard_map/ppermute | solution.py:25
  77.2 1.5 %collective-permute-start.6 = (f32[2,256,128]{2,1,0:T(8,128)S(1)}, f32[2,256,128]{2,1,0:T(8,128)S(1)}, u32[]{:S(2)}, u32[]{:S(2)}) collective-permute-start(f32[2,256,128]{2,1,0:T(8,128)S(1)} %get-tuple-element.46.rest_0_), channel_id=1, source_target_pairs={{0,2},{1,3},{2,0},{3,1},{4,6},{5,7},{6,4},{7,5},{8,10},{9,11},{10,... | collective-permute-start | bytes 786440 | tf_op jit(solution)/shard_map/ppermute | solution.py:25
  78.7 9.7 %collective-permute-done.10.other = f32[1032,128]{1,0:T(8,128)S(1)} collective-permute-done((f32[1032,128]{1,0:T(8,128)S(1)}, f32[1032,128]{1,0:T(8,128)S(1)}, u32[]{:S(2)}, u32[]{:S(2)}) %collective-permute-start.10) | collective-permute-done | bytes 528416 | tf_op jit(solution)/shard_map/ppermute | solution.py:25
  88.4 1.5 %shard_map.55 = (f32[512,128]{1,0:T(8,128)S(1)}, f32[512,128]{1,0:T(8,128)S(1)}) custom-call(s32[4]{0:T(128)S(1)} %copy-done.11, bf16[2,8,256,256]{3,2,1,0:T(8,128)(2,1)S(1)} %get-tuple-element.40.rest_0_.blocks, f32[1032,128]{1,0:T(8,128)S(1)} %shard_map.50.rest_0_.own, f32[1032,128]{1,0:T(8,128)S(1)} %collective-permute-done.10.other, ...), custom_call_target="tpu_custom_call" | custom-call | tf_op jit(solution)/shard_map/pallas_call | solution.py:312
  89.9 1.9 %collective-permute-start.18 = (f32[512,128]{1,0:T(8,128)S(1)}, f32[512,128]{1,0:T(8,128)S(1)}, u32[]{:S(2)}, u32[]{:S(2)}) collective-permute-start(f32[512,128]{1,0:T(8,128)S(1)} %get-tuple-element.49.rest_4_.rest_0_), channel_id=1, source_target_pairs={{0,4},{4,0},{8,12},{12,8},{16,20},{20,16},{24,28},{28,24},{1,5},{5... | collective-permute-start | bytes 786440 | tf_op jit(solution)/shard_map/ppermute | solution.py:25
  92.0 1.6 %shard_map.56 = (f32[2,256,128]{2,1,0:T(8,128)S(1)}, f32[2,256,128]{2,1,0:T(8,128)S(1)}) custom-call(bf16[1,8,256,256]{3,2,1,0:T(8,128)(2,1)S(1)} %get-tuple-element.39.blocks, bf16[1024,1024]{1,0:T(8,128)(2,1)S(1)} %shard_map.49.__2_.chosen, f32[512,128]{1,0:T(8,128)S(1)} %get-tuple-element.45.rest_4_.rest_0_, f32[512,128]{1,0:T(8,128)S(1)} %get-tuple-element.48.rest_1_, ...), custom_call_target="tpu_custom_call" | custom-call | tf_op jit(solution)/shard_map/pallas_call | solution.py:312
  93.6 1.5 %collective-permute-start.15 = (f32[2,256,128]{2,1,0:T(8,128)S(1)}, f32[2,256,128]{2,1,0:T(8,128)S(1)}, u32[]{:S(2)}, u32[]{:S(2)}) collective-permute-start(f32[2,256,128]{2,1,0:T(8,128)S(1)} %get-tuple-element.55), channel_id=1, source_target_pairs={{0,1},{1,0},{2,3},{3,2},{4,5},{5,4},{6,7},{7,6},{8,9},{9,8},{10,11... | collective-permute-start | bytes 786440 | tf_op jit(solution)/shard_map/ppermute | solution.py:25
  95.1 1.7 %collective-permute-done.7.rest_3_ = f32[2,256,128]{2,1,0:T(8,128)S(1)} collective-permute-done((f32[2,256,128]{2,1,0:T(8,128)S(1)}, f32[2,256,128]{2,1,0:T(8,128)S(1)}, u32[]{:S(2)}, u32[]{:S(2)}) %collective-permute-start.7) | collective-permute-done | bytes 262176 | tf_op jit(solution)/shard_map/ppermute | solution.py:25
  96.7 0.9 collective-permute-start.16
  97.6 1.5 %shard_map.57 = (f32[512,128]{1,0:T(8,128)S(1)}, f32[512,128]{1,0:T(8,128)S(1)}) custom-call(s32[4]{0:T(128)S(1)} %copy-done.11, bf16[2,8,256,256]{3,2,1,0:T(8,128)(2,1)S(1)} %copy-done.4, f32[2,256,128]{2,1,0:T(8,128)S(1)} %get-tuple-element.46.rest_0_, f32[2,256,128]{2,1,0:T(8,128)S(1)} %collective-permute-done.5.rest_1_, ...), custom_call_target="tpu_custom_call" | custom-call | tf_op jit(solution)/shard_map/pallas_call | solution.py:312
  99.2 1.0 collective-permute-start.17
  100.6 3.2 %collective-permute-done.19.rest_3_ = f32[512,128]{1,0:T(8,128)S(1)} collective-permute-done((f32[512,128]{1,0:T(8,128)S(1)}, f32[512,128]{1,0:T(8,128)S(1)}, u32[]{:S(2)}, u32[]{:S(2)}) %collective-permute-start.19) | collective-permute-done | bytes 262176 | tf_op jit(solution)/shard_map/ppermute | solution.py:25
  103.8 1.1 collective-permute-start.14
  104.9 1.5 %shard_map.58 = (f32[512,128]{1,0:T(8,128)S(1)}, f32[512,128]{1,0:T(8,128)S(1)}) custom-call(s32[4]{0:T(128)S(1)} %copy-done.11, bf16[2,8,256,256]{3,2,1,0:T(8,128)(2,1)S(1)} %get-tuple-element.40.rest_0_.blocks, f32[1032,128]{1,0:T(8,128)S(1)} %shard_map.52.rest_0_.own, f32[1032,128]{1,0:T(8,128)S(1)} %collective-permute-done.2.other, ...), custom_call_target="tpu_custom_call" | custom-call | tf_op jit(solution)/shard_map/pallas_call | solution.py:312
  106.4 1.9 %collective-permute-start.11 = (f32[512,128]{1,0:T(8,128)S(1)}, f32[512,128]{1,0:T(8,128)S(1)}, u32[]{:S(2)}, u32[]{:S(2)}) collective-permute-start(f32[512,128]{1,0:T(8,128)S(1)} %get-tuple-element.52.rest_4_.rest_0_), channel_id=1, source_target_pairs={{0,4},{4,0},{8,12},{12,8},{16,20},{20,16},{24,28},{28,24},{1,5},{5... | collective-permute-start | bytes 786440 | tf_op jit(solution)/shard_map/ppermute | solution.py:25
  108.5 1.6 %shard_map.59 = (f32[2,256,128]{2,1,0:T(8,128)S(1)}, f32[2,256,128]{2,1,0:T(8,128)S(1)}) custom-call(bf16[1,8,256,256]{3,2,1,0:T(8,128)(2,1)S(1)} %get-tuple-element.39.blocks, bf16[1024,1024]{1,0:T(8,128)(2,1)S(1)} %shard_map.49.__2_.chosen, f32[512,128]{1,0:T(8,128)S(1)} %get-tuple-element.49.rest_4_.rest_0_, f32[512,128]{1,0:T(8,128)S(1)} %get-tuple-element.56.rest_1_, ...), custom_call_target="tpu_custom_call" | custom-call | tf_op jit(solution)/shard_map/pallas_call | solution.py:312
  111.5 1.0 collective-permute-start.27
  112.5 1.7 %shard_map.60 = (f32[512,128]{1,0:T(8,128)S(1)}, f32[512,128]{1,0:T(8,128)S(1)}) custom-call(s32[4]{0:T(128)S(1)} %copy-done.11, bf16[2,8,256,256]{3,2,1,0:T(8,128)(2,1)S(1)} %copy-done.4, f32[2,256,128]{2,1,0:T(8,128)S(1)} %get-tuple-element.50.rest_4_.rest_0_, f32[2,256,128]{2,1,0:T(8,128)S(1)} %collective-permute-done.15.rest_1_, ...), custom_call_target="tpu_custom_call" | custom-call | tf_op jit(solution)/shard_map/pallas_call | solution.py:312
  114.2 1.5 %shard_map.61.rest_4_ = f32[1024,128]{1,0:T(8,128)S(1)} custom-call(s32[4]{0:T(128)S(1)} %copy-done.11, bf16[2,8,256,256]{3,2,1,0:T(8,128)(2,1)S(1)} %copy-done.2, f32[512,128]{1,0:T(8,128)S(1)} %get-tuple-element.51.rest_0_, f32[512,128]{1,0:T(8,128)S(1)} %get-tuple-element.54.rest_1_, f32[512,128]{1,0:T(8,128)S(1)} %collective-permute-done.13.rest_2_, ...), custom_call_target="tpu_custom_call" | custom-call | tf_op jit(solution)/shard_map/pallas_call | solution.py:312
  115.7 0.8 collective-permute-start.23
  116.6 3.9 %collective-permute-done.12.rest_3_ = f32[512,128]{1,0:T(8,128)S(1)} collective-permute-done((f32[512,128]{1,0:T(8,128)S(1)}, f32[512,128]{1,0:T(8,128)S(1)}, u32[]{:S(2)}, u32[]{:S(2)}) %collective-permute-start.12) | collective-permute-done | bytes 262176 | tf_op jit(solution)/shard_map/ppermute | solution.py:25
  120.5 1.6 %shard_map.62 = (f32[2,256,128]{2,1,0:T(8,128)S(1)}, f32[2,256,128]{2,1,0:T(8,128)S(1)}) custom-call(bf16[1,8,256,256]{3,2,1,0:T(8,128)(2,1)S(1)} %get-tuple-element.39.blocks, bf16[1024,1024]{1,0:T(8,128)(2,1)S(1)} %shard_map.49.__2_.chosen, f32[512,128]{1,0:T(8,128)S(1)} %get-tuple-element.52.rest_4_.rest_0_, f32[512,128]{1,0:T(8,128)S(1)} %get-tuple-element.53.rest_1_, ...), custom_call_target="tpu_custom_call" | custom-call | tf_op jit(solution)/shard_map/pallas_call | solution.py:312
  122.6 1.6 %collective-permute-start.21 = (f32[2,256,128]{2,1,0:T(8,128)S(1)}, f32[2,256,128]{2,1,0:T(8,128)S(1)}, u32[]{:S(2)}, u32[]{:S(2)}) collective-permute-start(f32[2,256,128]{2,1,0:T(8,128)S(1)} %get-tuple-element.59.rest_4_.rest_0_), channel_id=1, source_target_pairs={{0,2},{1,3},{2,0},{3,1},{4,6},{5,7},{6,4},{7,5},{8,10},{9,11},{10,... | collective-permute-start | bytes 786440 | tf_op jit(solution)/shard_map/ppermute | solution.py:25
  124.2 1.0 collective-permute-start.22
  125.2 1.5 %shard_map.63 = (f32[512,128]{1,0:T(8,128)S(1)}, f32[512,128]{1,0:T(8,128)S(1)}) custom-call(s32[4]{0:T(128)S(1)} %copy-done.11, bf16[2,8,256,256]{3,2,1,0:T(8,128)(2,1)S(1)} %copy-done.4, f32[2,256,128]{2,1,0:T(8,128)S(1)} %get-tuple-element.57.rest_4_.rest_0_, f32[2,256,128]{2,1,0:T(8,128)S(1)} %collective-permute-done.25.rest_1_, ...), custom_call_target="tpu_custom_call" | custom-call | tf_op jit(solution)/shard_map/pallas_call | solution.py:312
  127.3 1.5 %shard_map.64.rest_4_.rest_5_ = f32[1024,128]{1,0:T(8,128)S(1)} custom-call(s32[4]{0:T(128)S(1)} %copy-done.11, bf16[2,8,256,256]{3,2,1,0:T(8,128)(2,1)S(1)} %copy-done.2, f32[512,128]{1,0:T(8,128)S(1)} %get-tuple-element.58.rest_4_.rest_0_, f32[512,128]{1,0:T(8,128)S(1)} %get-tuple-element.61.rest_1_, f32[512,128]{1,0:T(8,128)S(1)} %collective-permute-done.23.rest_2_, ...), custom_call_target="tpu_custom_call" | custom-call | tf_op jit(solution)/shard_map/pallas_call | solution.py:312
  128.8 3.0 %collective-permute-done.21.rest_2_ = f32[2,256,128]{2,1,0:T(8,128)S(1)} collective-permute-done((f32[2,256,128]{2,1,0:T(8,128)S(1)}, f32[2,256,128]{2,1,0:T(8,128)S(1)}, u32[]{:S(2)}, u32[]{:S(2)}) %collective-permute-start.21) | collective-permute-done | bytes 262176 | tf_op jit(solution)/shard_map/ppermute | solution.py:25
  131.8 3.9 %collective-permute-done.22.rest_3_ = f32[2,256,128]{2,1,0:T(8,128)S(1)} collective-permute-done((f32[2,256,128]{2,1,0:T(8,128)S(1)}, f32[2,256,128]{2,1,0:T(8,128)S(1)}, u32[]{:S(2)}, u32[]{:S(2)}) %collective-permute-start.22) | collective-permute-done | bytes 262176 | tf_op jit(solution)/shard_map/ppermute | solution.py:25
  135.7 1.5 %shard_map.65 = (f32[512,128]{1,0:T(8,128)S(1)}, f32[512,128]{1,0:T(8,128)S(1)}) custom-call(s32[4]{0:T(128)S(1)} %copy-done.11, bf16[2,8,256,256]{3,2,1,0:T(8,128)(2,1)S(1)} %copy-done.4, f32[2,256,128]{2,1,0:T(8,128)S(1)} %get-tuple-element.59.rest_4_.rest_0_, f32[2,256,128]{2,1,0:T(8,128)S(1)} %collective-permute-done.20.rest_1_, ...), custom_call_target="tpu_custom_call" | custom-call | tf_op jit(solution)/shard_map/pallas_call | solution.py:312
  138.0 1.5 %shard_map.66.rest_6_.rest_7_ = f32[1024,128]{1,0:T(8,128)S(1)} custom-call(s32[4]{0:T(128)S(1)} %copy-done.11, bf16[2,8,256,256]{3,2,1,0:T(8,128)(2,1)S(1)} %copy-done.2, f32[512,128]{1,0:T(8,128)S(1)} %get-tuple-element.63.rest_4_.rest_0_, f32[512,128]{1,0:T(8,128)S(1)} %get-tuple-element.66.rest_1_, f32[512,128]{1,0:T(8,128)S(1)} %collective-permute-done.30.rest_2_, ...), custom_call_target="tpu_custom_call" | custom-call | tf_op jit(solution)/shard_map/pallas_call | solution.py:312
  139.6 2.6 %shard_map.67 = f32[8,128,512]{2,1,0:T(8,128)} custom-call(s32[4]{0:T(128)S(1)} %copy-done.11, bf16[2,8,256,256]{3,2,1,0:T(8,128)(2,1)S(1)} %copy-done.2, f32[512,128]{1,0:T(8,128)S(1)} %get-tuple-element.64.rest_4_.rest_0_, f32[512,128]{1,0:T(8,128)S(1)} %get-tuple-element.65.rest_1_, f32[512,128]{1,0:T(8,128)S(1)} %collective-permute-done.28.rest_2_, ...), custom_call_target="tpu_custom_call" | custom-call | tf_op jit(solution)/shard_map/pallas_call | solution.py:312
  (65 shorter events, 5.2 us)
Async XLA Ops:
  3.3 39.9 %collective-permute-start.1 = (f32[1032,128]{1,0:T(8,128)}, f32[1032,128]{1,0:T(8,128)}, u32[]{:S(2)}, u32[]{:S(2)}) collective-permute-start(f32[1032,128]{1,0:T(8,128)} %shard_map.46.rest_0_.own), channel_id=1, source_target_pairs={{0,16},{4,20},{8,24},{12,28},{16,0},{20,4},{24,8},{28,12},{1,17},{... | collective-permute-start | bytes 1585160 | tf_op jit(solution)/shard_map/ppermute | solution.py:25
  12.0 53.9 %collective-permute-start = (f32[1032,128]{1,0:T(8,128)}, f32[1032,128]{1,0:T(8,128)}, u32[]{:S(2)}, u32[]{:S(2)}) collective-permute-start(f32[1032,128]{1,0:T(8,128)} %get-tuple-element.36.rest_0_.own), channel_id=1, source_target_pairs={{0,16},{4,20},{8,24},{12,28},{16,0},{20,4},{24,8},{28,12},{1,17},{... | collective-permute-start | bytes 1585160 | tf_op jit(solution)/shard_map/ppermute | solution.py:25
  12.1 3.4 %copy-start = (f32[8,8,128,256]{3,2,1,0:T(8,128)S(1)}, f32[8,8,128,256]{3,2,1,0:T(8,128)}, u32[]{:S(2)}) copy-start(f32[8,8,128,256]{3,2,1,0:T(8,128)} %g_hbm.5) | copy-start | bytes 25165828
  15.4 1.0 copy-start.8
  16.5 4.3 %copy-start.12 = (s32[1024]{0:T(1024)S(1)}, s32[1024]{0:T(1024)}, u32[]{:S(2)}) copy-start(s32[1024]{0:T(1024)} %param.7) | copy-start | bytes 12292
  18.1 1.3 copy-start.1
  19.4 1.3 copy-start.3
  21.8 1.0 copy-start.10
  22.9 20.4 %copy-start.7 = (f32[1032,128]{1,0:T(8,128)S(1)}, f32[1032,128]{1,0:T(8,128)}, u32[]{:S(2)}) copy-start(f32[1032,128]{1,0:T(8,128)} %get-tuple-element.42.__0_) | copy-start | bytes 1585156
  23.3 20.1 %copy-start.5 = (f32[1032,128]{1,0:T(8,128)S(1)}, f32[1032,128]{1,0:T(8,128)}, u32[]{:S(2)}) copy-start(f32[1032,128]{1,0:T(8,128)} %shard_map.46.rest_0_.own) | copy-start | bytes 1585156
  23.3 20.1 %copy-start.11 = (s32[4]{0:T(128)S(1)}, s32[4]{0:T(128)}, u32[]{:S(2)}) copy-start(s32[4]{0:T(128)} %bits.27) | copy-start | bytes 52
  43.3 22.6 %copy-start.6 = (f32[1032,128]{1,0:T(8,128)S(1)}, f32[1032,128]{1,0:T(8,128)}, u32[]{:S(2)}) copy-start(f32[1032,128]{1,0:T(8,128)} %get-tuple-element.41.__0_) | copy-start | bytes 1585156
  43.3 22.6 %copy-start.9 = (f32[1032,128]{1,0:T(8,128)S(1)}, f32[1032,128]{1,0:T(8,128)}, u32[]{:S(2)}) copy-start(f32[1032,128]{1,0:T(8,128)} %get-tuple-element.36.rest_0_.own) | copy-start | bytes 1585156
  43.3 45.2 %collective-permute-start.10 = (f32[1032,128]{1,0:T(8,128)S(1)}, f32[1032,128]{1,0:T(8,128)S(1)}, u32[]{:S(2)}, u32[]{:S(2)}) collective-permute-start(f32[1032,128]{1,0:T(8,128)S(1)} %shard_map.50.rest_0_.own), channel_id=1, source_target_pairs={{0,16},{4,20},{8,24},{12,28},{16,0},{20,4},{24,8},{28,12},{1,17},{... | collective-permute-start | bytes 1585160 | tf_op jit(solution)/shard_map/ppermute | solution.py:25
  45.4 24.4 %collective-permute-start.3 = (f32[512,128]{1,0:T(8,128)S(1)}, f32[512,128]{1,0:T(8,128)S(1)}, u32[]{:S(2)}, u32[]{:S(2)}) collective-permute-start(f32[512,128]{1,0:T(8,128)S(1)} %get-tuple-element.43.__2_.rest_0_), channel_id=1, source_target_pairs={{0,4},{4,0},{8,12},{12,8},{16,20},{20,16},{24,28},{28,24},{1,5},{5... | collective-permute-start | bytes 786440 | tf_op jit(solution)/shard_map/ppermute | solution.py:25
  47.4 22.7 %collective-permute-start.4 = (f32[512,128]{1,0:T(8,128)S(1)}, f32[512,128]{1,0:T(8,128)S(1)}, u32[]{:S(2)}, u32[]{:S(2)}) collective-permute-start(f32[512,128]{1,0:T(8,128)S(1)} %get-tuple-element.44.rest_1_), channel_id=1, source_target_pairs={{0,4},{4,0},{8,12},{12,8},{16,20},{20,16},{24,28},{28,24},{1,5},{5... | collective-permute-start | bytes 786440 | tf_op jit(solution)/shard_map/ppermute | solution.py:25
  65.9 33.3 %collective-permute-start.2 = (f32[1032,128]{1,0:T(8,128)S(1)}, f32[1032,128]{1,0:T(8,128)S(1)}, u32[]{:S(2)}, u32[]{:S(2)}) collective-permute-start(f32[1032,128]{1,0:T(8,128)S(1)} %shard_map.52.rest_0_.own), channel_id=1, source_target_pairs={{0,16},{4,20},{8,24},{12,28},{16,0},{20,4},{24,8},{28,12},{1,17},{... | collective-permute-start | bytes 1585160 | tf_op jit(solution)/shard_map/ppermute | solution.py:25
  67.9 9.3 %collective-permute-start.8 = (f32[512,128]{1,0:T(8,128)S(1)}, f32[512,128]{1,0:T(8,128)S(1)}, u32[]{:S(2)}, u32[]{:S(2)}) collective-permute-start(f32[512,128]{1,0:T(8,128)S(1)} %get-tuple-element.45.rest_4_.rest_0_), channel_id=1, source_target_pairs={{0,4},{4,0},{8,12},{12,8},{16,20},{20,16},{24,28},{28,24},{1,5},{5... | collective-permute-start | bytes 786440 | tf_op jit(solution)/shard_map/ppermute | solution.py:25
  69.9 20.1 %collective-permute-start.9 = (f32[512,128]{1,0:T(8,128)S(1)}, f32[512,128]{1,0:T(8,128)S(1)}, u32[]{:S(2)}, u32[]{:S(2)}) collective-permute-start(f32[512,128]{1,0:T(8,128)S(1)} %get-tuple-element.48.rest_1_), channel_id=1, source_target_pairs={{0,4},{4,0},{8,12},{12,8},{16,20},{20,16},{24,28},{28,24},{1,5},{5... | collective-permute-start | bytes 786440 | tf_op jit(solution)/shard_map/ppermute | solution.py:25
  71.6 20.3 %collective-permute-start.5 = (f32[2,256,128]{2,1,0:T(8,128)S(1)}, f32[2,256,128]{2,1,0:T(8,128)S(1)}, u32[]{:S(2)}, u32[]{:S(2)}) collective-permute-start(f32[2,256,128]{2,1,0:T(8,128)S(1)} %get-tuple-element.47), channel_id=1, source_target_pairs={{0,1},{1,0},{2,3},{3,2},{4,5},{5,4},{6,7},{7,6},{8,9},{9,8},{10,11... | collective-permute-start | bytes 786440 | tf_op jit(solution)/shard_map/ppermute | solution.py:25
  77.2 16.4 %collective-permute-start.6 = (f32[2,256,128]{2,1,0:T(8,128)S(1)}, f32[2,256,128]{2,1,0:T(8,128)S(1)}, u32[]{:S(2)}, u32[]{:S(2)}) collective-permute-start(f32[2,256,128]{2,1,0:T(8,128)S(1)} %get-tuple-element.46.rest_0_), channel_id=1, source_target_pairs={{0,2},{1,3},{2,0},{3,1},{4,6},{5,7},{6,4},{7,5},{8,10},{9,11},{10,... | collective-permute-start | bytes 786440 | tf_op jit(solution)/shard_map/ppermute | solution.py:25
  88.4 8.3 %collective-permute-start.7 = (f32[2,256,128]{2,1,0:T(8,128)S(1)}, f32[2,256,128]{2,1,0:T(8,128)S(1)}, u32[]{:S(2)}, u32[]{:S(2)}) collective-permute-start(f32[2,256,128]{2,1,0:T(8,128)S(1)} %get-tuple-element.47), channel_id=1, source_target_pairs={{0,3},{1,2},{2,1},{3,0},{4,7},{5,6},{6,5},{7,4},{8,11},{9,10},{10,... | collective-permute-start | bytes 786440 | tf_op jit(solution)/shard_map/ppermute | solution.py:25
  89.9 10.2 %collective-permute-start.18 = (f32[512,128]{1,0:T(8,128)S(1)}, f32[512,128]{1,0:T(8,128)S(1)}, u32[]{:S(2)}, u32[]{:S(2)}) collective-permute-start(f32[512,128]{1,0:T(8,128)S(1)} %get-tuple-element.49.rest_4_.rest_0_), channel_id=1, source_target_pairs={{0,4},{4,0},{8,12},{12,8},{16,20},{20,16},{24,28},{28,24},{1,5},{5... | collective-permute-start | bytes 786440 | tf_op jit(solution)/shard_map/ppermute | solution.py:25
  91.9 5.7 %copy-start.4 = (bf16[2,8,256,256]{3,2,1,0:T(8,128)(2,1)S(1)}, bf16[2,8,256,256]{3,2,1,0:T(8,128)(2,1)}, u32[]{:S(2)}) copy-start(bf16[2,8,256,256]{3,2,1,0:T(8,128)(2,1)} %copy-done.3) | copy-start | bytes 6291460
  91.9 12.0 %collective-permute-start.19 = (f32[512,128]{1,0:T(8,128)S(1)}, f32[512,128]{1,0:T(8,128)S(1)}, u32[]{:S(2)}, u32[]{:S(2)}) collective-permute-start(f32[512,128]{1,0:T(8,128)S(1)} %get-tuple-element.56.rest_1_), channel_id=1, source_target_pairs={{0,4},{4,0},{8,12},{12,8},{16,20},{20,16},{24,28},{28,24},{1,5},{5... | collective-permute-start | bytes 786440 | tf_op jit(solution)/shard_map/ppermute | solution.py:25
  93.6 12.8 %collective-permute-start.15 = (f32[2,256,128]{2,1,0:T(8,128)S(1)}, f32[2,256,128]{2,1,0:T(8,128)S(1)}, u32[]{:S(2)}, u32[]{:S(2)}) collective-permute-start(f32[2,256,128]{2,1,0:T(8,128)S(1)} %get-tuple-element.55), channel_id=1, source_target_pairs={{0,1},{1,0},{2,3},{3,2},{4,5},{5,4},{6,7},{7,6},{8,9},{9,8},{10,11... | collective-permute-start | bytes 786440 | tf_op jit(solution)/shard_map/ppermute | solution.py:25
  96.7 11.6 %collective-permute-start.16 = (f32[2,256,128]{2,1,0:T(8,128)S(1)}, f32[2,256,128]{2,1,0:T(8,128)S(1)}, u32[]{:S(2)}, u32[]{:S(2)}) collective-permute-start(f32[2,256,128]{2,1,0:T(8,128)S(1)} %get-tuple-element.50.rest_4_.rest_0_), channel_id=1, source_target_pairs={{0,2},{1,3},{2,0},{3,1},{4,6},{5,7},{6,4},{7,5},{8,10},{9,11},{10,... | collective-permute-start | bytes 786440 | tf_op jit(solution)/shard_map/ppermute | solution.py:25
  99.2 11.3 %collective-permute-start.17 = (f32[2,256,128]{2,1,0:T(8,128)S(1)}, f32[2,256,128]{2,1,0:T(8,128)S(1)}, u32[]{:S(2)}, u32[]{:S(2)}) collective-permute-start(f32[2,256,128]{2,1,0:T(8,128)S(1)} %get-tuple-element.55), channel_id=1, source_target_pairs={{0,3},{1,2},{2,1},{3,0},{4,7},{5,6},{6,5},{7,4},{8,11},{9,10},{10,... | collective-permute-start | bytes 786440 | tf_op jit(solution)/shard_map/ppermute | solution.py:25
  100.1 11.0 %collective-permute-start.13 = (f32[512,128]{1,0:T(8,128)S(1)}, f32[512,128]{1,0:T(8,128)S(1)}, u32[]{:S(2)}, u32[]{:S(2)}) collective-permute-start(f32[512,128]{1,0:T(8,128)S(1)} %get-tuple-element.51.rest_0_), channel_id=1, source_target_pairs={{0,1},{1,0},{2,3},{3,2},{4,5},{5,4},{6,7},{7,6},{8,9},{9,8},{10,11... | collective-permute-start | bytes 786440 | tf_op jit(solution)/shard_map/ppermute | solution.py:25
  103.8 7.6 %collective-permute-start.14 = (f32[512,128]{1,0:T(8,128)S(1)}, f32[512,128]{1,0:T(8,128)S(1)}, u32[]{:S(2)}, u32[]{:S(2)}) collective-permute-start(f32[512,128]{1,0:T(8,128)S(1)} %get-tuple-element.54.rest_1_), channel_id=1, source_target_pairs={{0,1},{1,0},{2,3},{3,2},{4,5},{5,4},{6,7},{7,6},{8,9},{9,8},{10,11... | collective-permute-start | bytes 786440 | tf_op jit(solution)/shard_map/ppermute | solution.py:25
  106.4 9.3 %collective-permute-start.11 = (f32[512,128]{1,0:T(8,128)S(1)}, f32[512,128]{1,0:T(8,128)S(1)}, u32[]{:S(2)}, u32[]{:S(2)}) collective-permute-start(f32[512,128]{1,0:T(8,128)S(1)} %get-tuple-element.52.rest_4_.rest_0_), channel_id=1, source_target_pairs={{0,4},{4,0},{8,12},{12,8},{16,20},{20,16},{24,28},{28,24},{1,5},{5... | collective-permute-start | bytes 786440 | tf_op jit(solution)/shard_map/ppermute | solution.py:25
  108.4 12.1 %collective-permute-start.12 = (f32[512,128]{1,0:T(8,128)S(1)}, f32[512,128]{1,0:T(8,128)S(1)}, u32[]{:S(2)}, u32[]{:S(2)}) collective-permute-start(f32[512,128]{1,0:T(8,128)S(1)} %get-tuple-element.53.rest_1_), channel_id=1, source_target_pairs={{0,4},{4,0},{8,12},{12,8},{16,20},{20,16},{24,28},{28,24},{1,5},{5... | collective-permute-start | bytes 786440 | tf_op jit(solution)/shard_map/ppermute | solution.py:25
  110.1 4.1 %copy-start.2 = (bf16[2,8,256,256]{3,2,1,0:T(8,128)(2,1)S(1)}, bf16[2,8,256,256]{3,2,1,0:T(8,128)(2,1)}, u32[]{:S(2)}) copy-start(bf16[2,8,256,256]{3,2,1,0:T(8,128)(2,1)} %copy-done.1) | copy-start | bytes 6291460
  110.5 11.5 %collective-permute-start.25 = (f32[2,256,128]{2,1,0:T(8,128)S(1)}, f32[2,256,128]{2,1,0:T(8,128)S(1)}, u32[]{:S(2)}, u32[]{:S(2)}) collective-permute-start(f32[2,256,128]{2,1,0:T(8,128)S(1)} %get-tuple-element.62), channel_id=1, source_target_pairs={{0,1},{1,0},{2,3},{3,2},{4,5},{5,4},{6,7},{7,6},{8,9},{9,8},{10,11... | collective-permute-start | bytes 786440 | tf_op jit(solution)/shard_map/ppermute | solution.py:25
  111.1 11.5 %collective-permute-start.26 = (f32[2,256,128]{2,1,0:T(8,128)S(1)}, f32[2,256,128]{2,1,0:T(8,128)S(1)}, u32[]{:S(2)}, u32[]{:S(2)}) collective-permute-start(f32[2,256,128]{2,1,0:T(8,128)S(1)} %get-tuple-element.57.rest_4_.rest_0_), channel_id=1, source_target_pairs={{0,2},{1,3},{2,0},{3,1},{4,6},{5,7},{6,4},{7,5},{8,10},{9,11},{10,... | collective-permute-start | bytes 786440 | tf_op jit(solution)/shard_map/ppermute | solution.py:25
  111.5 12.7 %collective-permute-start.27 = (f32[2,256,128]{2,1,0:T(8,128)S(1)}, f32[2,256,128]{2,1,0:T(8,128)S(1)}, u32[]{:S(2)}, u32[]{:S(2)}) collective-permute-start(f32[2,256,128]{2,1,0:T(8,128)S(1)} %get-tuple-element.62), channel_id=1, source_target_pairs={{0,3},{1,2},{2,1},{3,0},{4,7},{5,6},{6,5},{7,4},{8,11},{9,10},{10,... | collective-permute-start | bytes 786440 | tf_op jit(solution)/shard_map/ppermute | solution.py:25
  115.7 11.0 %collective-permute-start.23 = (f32[512,128]{1,0:T(8,128)S(1)}, f32[512,128]{1,0:T(8,128)S(1)}, u32[]{:S(2)}, u32[]{:S(2)}) collective-permute-start(f32[512,128]{1,0:T(8,128)S(1)} %get-tuple-element.58.rest_4_.rest_0_), channel_id=1, source_target_pairs={{0,1},{1,0},{2,3},{3,2},{4,5},{5,4},{6,7},{7,6},{8,9},{9,8},{10,11... | collective-permute-start | bytes 786440 | tf_op jit(solution)/shard_map/ppermute | solution.py:25
  120.5 6.5 %collective-permute-start.24 = (f32[512,128]{1,0:T(8,128)S(1)}, f32[512,128]{1,0:T(8,128)S(1)}, u32[]{:S(2)}, u32[]{:S(2)}) collective-permute-start(f32[512,128]{1,0:T(8,128)S(1)} %get-tuple-element.61.rest_1_), channel_id=1, source_target_pairs={{0,1},{1,0},{2,3},{3,2},{4,5},{5,4},{6,7},{7,6},{8,9},{9,8},{10,11... | collective-permute-start | bytes 786440 | tf_op jit(solution)/shard_map/ppermute | solution.py:25
  122.0 6.7 %collective-permute-start.20 = (f32[2,256,128]{2,1,0:T(8,128)S(1)}, f32[2,256,128]{2,1,0:T(8,128)S(1)}, u32[]{:S(2)}, u32[]{:S(2)}) collective-permute-start(f32[2,256,128]{2,1,0:T(8,128)S(1)} %get-tuple-element.60), channel_id=1, source_target_pairs={{0,1},{1,0},{2,3},{3,2},{4,5},{5,4},{6,7},{7,6},{8,9},{9,8},{10,11... | collective-permute-start | bytes 786440 | tf_op jit(solution)/shard_map/ppermute | solution.py:25
  122.6 9.2 %collective-permute-start.21 = (f32[2,256,128]{2,1,0:T(8,128)S(1)}, f32[2,256,128]{2,1,0:T(8,128)S(1)}, u32[]{:S(2)}, u32[]{:S(2)}) collective-permute-start(f32[2,256,128]{2,1,0:T(8,128)S(1)} %get-tuple-element.59.rest_4_.rest_0_), channel_id=1, source_target_pairs={{0,2},{1,3},{2,0},{3,1},{4,6},{5,7},{6,4},{7,5},{8,10},{9,11},{10,... | collective-permute-start | bytes 786440 | tf_op jit(solution)/shard_map/ppermute | solution.py:25
  124.2 11.5 %collective-permute-start.22 = (f32[2,256,128]{2,1,0:T(8,128)S(1)}, f32[2,256,128]{2,1,0:T(8,128)S(1)}, u32[]{:S(2)}, u32[]{:S(2)}) collective-permute-start(f32[2,256,128]{2,1,0:T(8,128)S(1)} %get-tuple-element.60), channel_id=1, source_target_pairs={{0,3},{1,2},{2,1},{3,0},{4,7},{5,6},{6,5},{7,4},{8,11},{9,10},{10,... | collective-permute-start | bytes 786440 | tf_op jit(solution)/shard_map/ppermute | solution.py:25
  126.7 11.3 %collective-permute-start.30 = (f32[512,128]{1,0:T(8,128)S(1)}, f32[512,128]{1,0:T(8,128)S(1)}, u32[]{:S(2)}, u32[]{:S(2)}) collective-permute-start(f32[512,128]{1,0:T(8,128)S(1)} %get-tuple-element.63.rest_4_.rest_0_), channel_id=1, source_target_pairs={{0,1},{1,0},{2,3},{3,2},{4,5},{5,4},{6,7},{7,6},{8,9},{9,8},{10,11... | collective-permute-start | bytes 786440 | tf_op jit(solution)/shard_map/ppermute | solution.py:25
  127.0 11.0 %collective-permute-start.31 = (f32[512,128]{1,0:T(8,128)S(1)}, f32[512,128]{1,0:T(8,128)S(1)}, u32[]{:S(2)}, u32[]{:S(2)}) collective-permute-start(f32[512,128]{1,0:T(8,128)S(1)} %get-tuple-element.66.rest_1_), channel_id=1, source_target_pairs={{0,1},{1,0},{2,3},{3,2},{4,5},{5,4},{6,7},{7,6},{8,9},{9,8},{10,11... | collective-permute-start | bytes 786440 | tf_op jit(solution)/shard_map/ppermute | solution.py:25
  137.2 2.3 %collective-permute-start.28 = (f32[512,128]{1,0:T(8,128)S(1)}, f32[512,128]{1,0:T(8,128)S(1)}, u32[]{:S(2)}, u32[]{:S(2)}) collective-permute-start(f32[512,128]{1,0:T(8,128)S(1)} %get-tuple-element.64.rest_4_.rest_0_), channel_id=1, source_target_pairs={{0,1},{1,0},{2,3},{3,2},{4,5},{5,4},{6,7},{7,6},{8,9},{9,8},{10,11... | collective-permute-start | bytes 786440 | tf_op jit(solution)/shard_map/ppermute | solution.py:25
  138.0 1.6 %collective-permute-start.29 = (f32[512,128]{1,0:T(8,128)S(1)}, f32[512,128]{1,0:T(8,128)S(1)}, u32[]{:S(2)}, u32[]{:S(2)}) collective-permute-start(f32[512,128]{1,0:T(8,128)S(1)} %get-tuple-element.65.rest_1_), channel_id=1, source_target_pairs={{0,1},{1,0},{2,3},{3,2},{4,5},{5,4},{6,7},{7,6},{8,9},{9,8},{10,11... | collective-permute-start | bytes 786440 | tf_op jit(solution)/shard_map/ppermute | solution.py:25
where the time goes:
time: 143 us; the launch traced here: 142 us
  waiting for transfers between devices  69.7 us (49%)
  Pallas kernels  36.6 us (26%)
  starting transfers between devices  26.3 us (18%)
  local copies, waits for them, and re-layouts  9.18 us (6%)
    ppermute x32, waiting for transfers between devices, partner_2(): lax.ppermute(shard, axis, [(i, i ^ mask) for i in range(lax.axis_size(axi...  69.7 us
    pallas_call x22, Pallas kernels, run(): pl.pallas_call(kernel, out_shape=out_shape, in_specs=list(in_specs) + [AN...  36.6 us
    ppermute x32, starting transfers between devices, partner_2(): lax.ppermute(shard, axis, [(i, i ^ mask) for i in range(lax.axis_size(axi...  26.3 us
    unnamed x26, local copies, waits for them, and re-layouts  8.15 us
  transfers between devices with their start and end apart: 32, of which 10 were waited for; matrix products, arithmetic and copies ran while one was open for 1% of the time, Pallas kernels for 22%

commit v1 on v0

--- a/solution.py
+++ b/solution.py
@@ -11,11 +11,11 @@
 GROUP = 128
 CUTS = (1, 1, 1, 1)
 PAD = 8
-PAD_X = 8
-WINDOW = 2
-CORE_SPLIT = 2
-Y_CUTS = (2, 2, 2, 2)
-JOINT = 0
+PAD_X = 0
+LAG = (0, 2, 2, 2)
+CORE_SPLIT = 1
+Y_CUTS = (2, 2, 2, 1)
+JOINT = 3
 STAGES = (1, 3, 4, 6)
 VMEM_LIMIT = 16 * 1024 * 1024
 FIRST_LIMIT = 62 * 1024 * 1024
@@ -28,13 +28,6 @@
 def split2(x):
     high = x.astype(BF16)
     return high, (x - high.astype(F32)).astype(BF16)
-
-
-def split3(x):
-    high = x.astype(BF16)
-    rest = x - high.astype(F32)
-    middle = rest.astype(BF16)
-    return high, middle, (rest - middle.astype(F32)).astype(BF16)
 
 
 def product(blocks, x):
@@ -140,6 +133,10 @@
     pass
 
 
+def cross_kernel(joint, *rest):
+    rest[-1][...] = joint[1]
+
+
 def prepare_kernel(g_hbm, *rest):
     outs, (g_ref, arrived) = rest[-2 - len(STAGES):-2], rest[-2:]
     levels, nodes, rank, _ = g_ref.shape
@@ -247,10 +244,10 @@
     outs = [[rest[-3].at[offset]] for offset in range(count)] if joint else [[ref] for ref in rest[-1 - count:-1]]
     if joint:
         outs[1 % count].append(rest[-2])
-    width = spread.shape[1] // 3
+    width = spread.shape[1] // 2
 
     def put(first, size, value):
-        spread[first:first + size] = jnp.concatenate(split3(value), axis=1)
+        spread[first:first + size] = jnp.concatenate(split2(value), axis=1)
 
     cross_level(
         put, axis, shift, blocks, level,
@@ -262,7 +259,7 @@
         for side in range(2):
             place = (index * 2 + side) * piece_rows
             out = jnp.dot(chosen[place:place + piece_rows], spread[...], preferred_element_type=F32)
-            out = (out[:, :width] + out[:, width:2 * width]) + out[:, 2 * width:]
+            out = out[:, :width] + out[:, width:]
             for target in targets:
                 pack(target.at[side, :piece_rows // parts], out, parts)
 
@@ -347,7 +344,7 @@
         )
         for offset, array in enumerate(out):
             store["whole", index + offset] = array
-        if index < WINDOW:
+        if not index or LAG[1] == 2:
             store["far", index] = partner_2(out[0], "src", src_far)
 
     def step_p(_):
@@ -381,7 +378,7 @@
             [ANY, ANY],
             [ANY],
             [],
-            [array, store["far", index - WINDOW]],
+            [array, store["far", index - LAG[index]]],
             aliases={0: 0},
         )[0]
         store["whole", index] = array
@@ -412,7 +409,7 @@
             [shape((tgt_far, 2, piece[1] + PAD_X, GROUP), F32), shape(piece, F32)] if joint else [shape(piece, F32)] * tgt_far,
             [VMEM] * (2 + 2 * cuts),
             [VMEM] * (2 if joint else tgt_far),
-            [pltpu.VMEM((rows, 3 * GROUP // parts), BF16)],
+            [pltpu.VMEM((rows, 2 * GROUP // parts), BF16)],
             [store["blocks", 3], store["chosen"], *store["own", index], *store["near", index]],
         )
         for offset, piece in enumerate(pieces):
@@ -437,7 +434,9 @@
     def step_s(index):
         if index < JOINT:
             for offset in range(2, n_tgt, 2):
-                store["moved", index, offset + 1] = partner_2(store["moved", index, offset][1], "tgt", 1)
+                joint = store["moved", index, offset]
+                cross = run(cross_kernel, [shape(joint.shape[1:], F32)], [VMEM], [VMEM], [], [joint])[0]
+                store["moved", index, offset + 1] = partner_2(cross, "tgt", 1)
 
     def step_d(index):
         _, _, parts = chunks[index]
@@ -513,8 +512,8 @@
     'A1',
     'P0',
     'Q0',
+    'B0',
     'R2',
-    'B0',
     'R3',
     'B1',
     'C0',
@@ -524,18 +523,22 @@
     'C1',
     'T1',
     'X1',
+    'S0',
     'D0',
-    'B3',
     'C2',
     'T2',
     'X2',
+    'B3',
+    'S1',
     'D1',
-    'E0',
+    'S2',
     'C3',
     'T3',
     'X3',
     'D2',
+    'E0',
     'E1',
+    'S3',
     'D3',
     'E2',
     'E3',

time: 143 us -> 137 us (0.958)
  starting transfers between devices: 26.3 us -> 20.4 us
  waiting for transfers between devices: 69.7 us -> 72.4 us
  Pallas kernels: 36.6 us -> 34.2 us
    ppermute x32 -> x27, starting transfers between devices: 26.3 us -> 20.4 us  [partner_2(): lax.ppermute(shard, axis, [(i, i ^ mask) for i in range(lax.axis_size(axi...]
    ppermute x32 -> x27, waiting for transfers between devices: 69.7 us -> 72.4 us  [partner_2(): lax.ppermute(shard, axis, [(i, i ^ mask) for i in range(lax.axis_size(axi...]
    pallas_call x22 -> x25, Pallas kernels: 36.6 us -> 34.2 us  [run(): pl.pallas_call(kernel, out_shape=out_shape, in_specs=list(in_specs) + [AN...]
  transfers between devices with their start and end apart: 32 -> 27, of which waited for: 10 -> 13; matrix products, arithmetic and copies ran while one was open for 1% -> 1% of each run, Pallas kernels for 22% -> 21%
where the time goes in v1:
time: 137 us
  waiting for transfers between devices  72.4 us (53%)
  Pallas kernels  34.2 us (25%)
  starting transfers between devices  20.4 us (15%)
  local copies, waits for them, and re-layouts  9.18 us (7%)
    ppermute x27, waiting for transfers between devices, partner_2(): lax.ppermute(shard, axis, [(i, i ^ mask) for i in range(lax.axis_size(axi...  72.4 us
    pallas_call x25, Pallas kernels, run(): pl.pallas_call(kernel, out_shape=out_shape, in_specs=list(in_specs) + [AN...  34.2 us
    ppermute x27, starting transfers between devices, partner_2(): lax.ppermute(shard, axis, [(i, i ^ mask) for i in range(lax.axis_size(axi...  20.4 us
    unnamed x26, local copies, waits for them, and re-layouts  8.14 us
  transfers between devices with their start and end apart: 27, of which 13 were waited for; matrix products, arithmetic and copies ran while one was open for 1% of the time, Pallas kernels for 21%

profile of v1, /device:TPU:0, one launch (start us, length us, event | category | flops | bytes accessed | tf_op | source)
XLA Modules:
  0.0 136.7 jit_solution(6400929678058417110)
XLA Ops:
  0.0 3.3 %shard_map.46.rest_0_.own = f32[1032,128]{1,0:T(8,128)} custom-call(s32[4]{0:T(128)} %bits.27, f32[8,128,512]{2,1,0:T(8,128)} %x_hbm.3, f32[8,8,128,256]{3,2,1,0:T(8,128)} %g_hbm.5), custom_call_target="tpu_custom_call" | custom-call | tf_op jit(solution)/shard_map/pallas_call | solution.py:309
  3.3 4.1 %collective-permute-start.1 = (f32[1032,128]{1,0:T(8,128)}, f32[1032,128]{1,0:T(8,128)}, u32[]{:S(2)}, u32[]{:S(2)}) collective-permute-start(f32[1032,128]{1,0:T(8,128)} %shard_map.46.rest_0_.own), channel_id=1, source_target_pairs={{0,16},{4,20},{8,24},{12,28},{16,0},{20,4},{24,8},{28,12},{1,17},{... | collective-permute-start | bytes 1585160 | tf_op jit(solution)/shard_map/ppermute | solution.py:25
  7.4 4.5 %shard_map.47 = (f32[1032,128]{1,0:T(8,128)}, f32[1032,128]{1,0:T(8,128)}, f32[1032,128]{1,0:T(8,128)}) custom-call(s32[4]{0:T(128)} %bits.27, f32[8,128,512]{2,1,0:T(8,128)} %x_hbm.3, f32[8,8,128,256]{3,2,1,0:T(8,128)} %g_hbm.5, f32[1032,128]{1,0:T(8,128)} %shard_map.46.rest_0_.own), custom_call_target="tpu_custom_call" | custom-call | tf_op jit(solution)/shard_map/pallas_call | solution.py:309
  12.0 3.4 %copy-done = f32[8,8,128,256]{3,2,1,0:T(8,128)S(1)} copy-done((f32[8,8,128,256]{3,2,1,0:T(8,128)S(1)}, f32[8,8,128,256]{3,2,1,0:T(8,128)}, u32[]{:S(2)}) %copy-start) | copy-done | bytes 8388632
  15.4 1.0 copy-done.8
  16.4 1.6 %shard_map.48 = (bf16[2,8,256,256]{3,2,1,0:T(8,128)(2,1)S(1)}, bf16[1,8,256,256]{3,2,1,0:T(8,128)(2,1)S(1)}, bf16[2,8,256,256]{3,2,1,0:T(8,128)(2,1)S(1)}, bf16[2,8,256,256]{3,2,1,0:T(8,128)(2,1)S(1)}) custom-call(f32[8,8,128,256]{3,2,1,0:T(8,128)S(1)} %copy-done, f32[1032,128]{1,0:T(8,128)S(1)} %copy-done.8), custom_call_target="tpu_custom_call" | custom-call | tf_op jit(solution)/shard_map/pallas_call | solution.py:309
  18.1 1.3 copy-done.1
  19.4 1.3 copy-done.3
  20.7 1.0 copy.7.relabel_ref
  21.8 1.0 copy-done.10
  23.2 20.0 %collective-permute-done.1.other.__1_ = f32[1032,128]{1,0:T(8,128)} collective-permute-done((f32[1032,128]{1,0:T(8,128)}, f32[1032,128]{1,0:T(8,128)}, u32[]{:S(2)}, u32[]{:S(2)}) %collective-permute-start.1) | collective-permute-done | bytes 528416 | tf_op jit(solution)/shard_map/ppermute | solution.py:25
  43.3 2.0 %shard_map.50 = (f32[512,128]{1,0:T(8,128)S(1)}, f32[512,128]{1,0:T(8,128)S(1)}) custom-call(s32[4]{0:T(128)S(1)} %copy-done.11, bf16[2,8,256,256]{3,2,1,0:T(8,128)(2,1)S(1)} %get-tuple-element.30.rest_0_.blocks, f32[1032,128]{1,0:T(8,128)S(1)} %copy-done.5, f32[1032,128]{1,0:T(8,128)} %collective-permute-done.1.other.__1_, ...), custom_call_target="tpu_custom_call" | custom-call | tf_op jit(solution)/shard_map/pallas_call | solution.py:309
  45.3 1.9 %collective-permute-start.4 = (f32[512,128]{1,0:T(8,128)S(1)}, f32[512,128]{1,0:T(8,128)S(1)}, u32[]{:S(2)}, u32[]{:S(2)}) collective-permute-start(f32[512,128]{1,0:T(8,128)S(1)} %get-tuple-element.33.__2_.rest_0_), channel_id=1, source_target_pairs={{0,4},{4,0},{8,12},{12,8},{16,20},{20,16},{24,28},{28,24},{1,5},{5... | collective-permute-start | bytes 786440 | tf_op jit(solution)/shard_map/ppermute | solution.py:25
  47.4 18.5 %collective-permute-done.__1_.other = f32[1032,128]{1,0:T(8,128)} collective-permute-done((f32[1032,128]{1,0:T(8,128)}, f32[1032,128]{1,0:T(8,128)}, u32[]{:S(2)}, u32[]{:S(2)}) %collective-permute-start) | collective-permute-done | bytes 528416 | tf_op jit(solution)/shard_map/ppermute | solution.py:25
  65.9 2.0 %shard_map.53 = (f32[512,128]{1,0:T(8,128)S(1)}, f32[512,128]{1,0:T(8,128)S(1)}) custom-call(s32[4]{0:T(128)S(1)} %copy-done.11, bf16[2,8,256,256]{3,2,1,0:T(8,128)(2,1)S(1)} %get-tuple-element.30.rest_0_.blocks, f32[1032,128]{1,0:T(8,128)S(1)} %copy-done.9, f32[1032,128]{1,0:T(8,128)} %collective-permute-done.__1_.other, f32[1032,128]{1,0:T(8,128)S(1)} %shard_map.52.rest_0_.own), custom_call_target="tpu_custom_call" | custom-call | tf_op jit(solution)/shard_map/pallas_call | solution.py:309
  67.9 1.0 shard_map.54
  68.9 1.9 %collective-permute-start.9 = (f32[2,2,256,128]{3,2,1,0:T(8,128)S(1)}, f32[2,2,256,128]{3,2,1,0:T(8,128)S(1)}, u32[]{:S(2)}, u32[]{:S(2)}) collective-permute-start(f32[2,2,256,128]{3,2,1,0:T(8,128)S(1)} %get-tuple-element.36.rest_0_), channel_id=1, source_target_pairs={{0,2},{1,3},{2,0},{3,1},{4,6},{5,7},{6,4},{7,5},{8,10},{9,11},{10,... | collective-permute-start | bytes 1572872 | tf_op jit(solution)/shard_map/ppermute | solution.py:25
  70.8 1.5 %collective-permute-start.10 = (f32[512,128]{1,0:T(8,128)S(1)}, f32[512,128]{1,0:T(8,128)S(1)}, u32[]{:S(2)}, u32[]{:S(2)}) collective-permute-start(f32[512,128]{1,0:T(8,128)S(1)} %get-tuple-element.35.rest_4_.rest_0_), channel_id=1, source_target_pairs={{0,4},{4,0},{8,12},{12,8},{16,20},{20,16},{24,28},{28,24},{1,5},{5... | collective-permute-start | bytes 786440 | tf_op jit(solution)/shard_map/ppermute | solution.py:25
  72.4 0.5 collective-permute-start.11
  72.9 3.4 %collective-permute-done.3.other = f32[1032,128]{1,0:T(8,128)S(1)} collective-permute-done((f32[1032,128]{1,0:T(8,128)S(1)}, f32[1032,128]{1,0:T(8,128)S(1)}, u32[]{:S(2)}, u32[]{:S(2)}) %collective-permute-start.3) | collective-permute-done | bytes 528416 | tf_op jit(solution)/shard_map/ppermute | solution.py:25
  76.3 1.5 %shard_map.55 = (f32[512,128]{1,0:T(8,128)S(1)}, f32[512,128]{1,0:T(8,128)S(1)}) custom-call(s32[4]{0:T(128)S(1)} %copy-done.11, bf16[2,8,256,256]{3,2,1,0:T(8,128)(2,1)S(1)} %get-tuple-element.30.rest_0_.blocks, f32[1032,128]{1,0:T(8,128)S(1)} %shard_map.51.__2_.own, f32[1032,128]{1,0:T(8,128)S(1)} %collective-permute-done.3.other, ...), custom_call_target="tpu_custom_call" | custom-call | tf_op jit(solution)/shard_map/pallas_call | solution.py:309
  77.8 1.7 %collective-permute-done.10.rest_2_ = f32[512,128]{1,0:T(8,128)S(1)} collective-permute-done((f32[512,128]{1,0:T(8,128)S(1)}, f32[512,128]{1,0:T(8,128)S(1)}, u32[]{:S(2)}, u32[]{:S(2)}) %collective-permute-start.10) | collective-permute-done | bytes 262176 | tf_op jit(solution)/shard_map/ppermute | solution.py:25
  79.5 1.5 %collective-permute-start.6 = (f32[512,128]{1,0:T(8,128)S(1)}, f32[512,128]{1,0:T(8,128)S(1)}, u32[]{:S(2)}, u32[]{:S(2)}) collective-permute-start(f32[512,128]{1,0:T(8,128)S(1)} %get-tuple-element.37.rest_4_.rest_0_), channel_id=1, source_target_pairs={{0,4},{4,0},{8,12},{12,8},{16,20},{20,16},{24,28},{28,24},{1,5},{5... | collective-permute-start | bytes 786440 | tf_op jit(solution)/shard_map/ppermute | solution.py:25
  81.0 3.7 %collective-permute-done.11.rest_3_ = f32[512,128]{1,0:T(8,128)S(1)} collective-permute-done((f32[512,128]{1,0:T(8,128)S(1)}, f32[512,128]{1,0:T(8,128)S(1)}, u32[]{:S(2)}, u32[]{:S(2)}) %collective-permute-start.11) | collective-permute-done | bytes 262176 | tf_op jit(solution)/shard_map/ppermute | solution.py:25
  84.7 1.0 shard_map.56
  86.2 1.5 %collective-permute-start.7 = (f32[512,128]{1,0:T(8,128)S(1)}, f32[512,128]{1,0:T(8,128)S(1)}, u32[]{:S(2)}, u32[]{:S(2)}) collective-permute-start(f32[512,128]{1,0:T(8,128)S(1)} %get-tuple-element.38.rest_1_), channel_id=1, source_target_pairs={{0,4},{4,0},{8,12},{12,8},{16,20},{20,16},{24,28},{28,24},{1,5},{5... | collective-permute-start | bytes 786440 | tf_op jit(solution)/shard_map/ppermute | solution.py:25
  87.8 1.5 %shard_map.58.rest_4_.rest_0_ = f32[1024,128]{1,0:T(8,128)S(1)} custom-call(s32[4]{0:T(128)S(1)} %copy-done.11, bf16[2,8,256,256]{3,2,1,0:T(8,128)(2,1)S(1)} %copy-done.4, f32[2,2,256,128]{3,2,1,0:T(8,128)S(1)} %get-tuple-element.36.rest_0_, f32[2,256,128]{2,1,0:T(8,128)S(1)} %collective-permute-done.8.rest_1_, ...), custom_call_target="tpu_custom_call" | custom-call | tf_op jit(solution)/shard_map/pallas_call | solution.py:309
  89.3 5.3 %collective-permute-done.7.rest_3_ = f32[512,128]{1,0:T(8,128)S(1)} collective-permute-done((f32[512,128]{1,0:T(8,128)S(1)}, f32[512,128]{1,0:T(8,128)S(1)}, u32[]{:S(2)}, u32[]{:S(2)}) %collective-permute-start.7) | collective-permute-done | bytes 262176 | tf_op jit(solution)/shard_map/ppermute | solution.py:25
  94.6 1.0 shard_map.59
  95.6 1.8 %collective-permute-start.14 = (f32[2,2,256,128]{3,2,1,0:T(8,128)S(1)}, f32[2,2,256,128]{3,2,1,0:T(8,128)S(1)}, u32[]{:S(2)}, u32[]{:S(2)}) collective-permute-start(f32[2,2,256,128]{3,2,1,0:T(8,128)S(1)} %get-tuple-element.42.rest_0_), channel_id=1, source_target_pairs={{0,2},{1,3},{2,0},{3,1},{4,6},{5,7},{6,4},{7,5},{8,10},{9,11},{10,... | collective-permute-start | bytes 1572872 | tf_op jit(solution)/shard_map/ppermute | solution.py:25
  97.4 4.3 %collective-permute-done.2.other = f32[1032,128]{1,0:T(8,128)S(1)} collective-permute-done((f32[1032,128]{1,0:T(8,128)S(1)}, f32[1032,128]{1,0:T(8,128)S(1)}, u32[]{:S(2)}, u32[]{:S(2)}) %collective-permute-start.2) | collective-permute-done | bytes 528416 | tf_op jit(solution)/shard_map/ppermute | solution.py:25
  101.7 1.5 %shard_map.60.rest_0_ = f32[1024,128]{1,0:T(8,128)S(1)} custom-call(s32[4]{0:T(128)S(1)} %copy-done.11, bf16[2,8,256,256]{3,2,1,0:T(8,128)(2,1)S(1)} %get-tuple-element.30.rest_0_.blocks, f32[1032,128]{1,0:T(8,128)S(1)} %shard_map.52.rest_0_.own, f32[1032,128]{1,0:T(8,128)S(1)} %collective-permute-done.2.other, f32[2,2,256,128]{3,2,1,0:T(8,128)S(1)} %get-tuple-element.42.rest_0_), custom_call_target="tpu_custom_call" | custom-call | tf_op jit(solution)/shard_map/pallas_call | solution.py:309
  103.2 1.3 collective-permute-start.13
  105.2 0.9 collective-permute-done.17.rest_3_
  106.1 1.5 %shard_map.62.rest_0_ = f32[1024,128]{1,0:T(8,128)S(1)} custom-call(s32[4]{0:T(128)S(1)} %copy-done.11, bf16[2,8,256,256]{3,2,1,0:T(8,128)(2,1)S(1)} %copy-done.4, f32[2,2,256,128]{3,2,1,0:T(8,128)S(1)} %get-tuple-element.41.rest_0_, f32[2,256,128]{2,1,0:T(8,128)S(1)} %collective-permute-done.15.rest_1_, ...), custom_call_target="tpu_custom_call" | custom-call | tf_op jit(solution)/shard_map/pallas_call | solution.py:309
  107.8 3.6 %collective-permute-done.14.joint.rest_2_ = f32[2,2,256,128]{3,2,1,0:T(8,128)S(1)} collective-permute-done((f32[2,2,256,128]{3,2,1,0:T(8,128)S(1)}, f32[2,2,256,128]{3,2,1,0:T(8,128)S(1)}, u32[]{:S(2)}, u32[]{:S(2)}) %collective-permute-start.14) | collective-permute-done | bytes 524320 | tf_op jit(solution)/shard_map/ppermute | solution.py:25
  111.5 3.9 %collective-permute-done.13.rest_1_ = f32[1024,128]{1,0:T(8,128)S(1)} collective-permute-done((f32[1024,128]{1,0:T(8,128)S(1)}, f32[1024,128]{1,0:T(8,128)S(1)}, u32[]{:S(2)}, u32[]{:S(2)}) %collective-permute-start.13) | collective-permute-done | bytes 524320 | tf_op jit(solution)/shard_map/ppermute | solution.py:25
  115.4 1.0 shard_map.64
  116.6 1.0 collective-permute-start.19
  117.6 0.8 collective-permute-start.20
  118.4 1.7 %shard_map.65.rest_2_.rest_0_ = f32[1024,128]{1,0:T(8,128)S(1)} custom-call(s32[4]{0:T(128)S(1)} %copy-done.11, bf16[2,8,256,256]{3,2,1,0:T(8,128)(2,1)S(1)} %copy-done.4, f32[2,2,256,128]{3,2,1,0:T(8,128)S(1)} %get-tuple-element.42.rest_0_, f32[2,256,128]{2,1,0:T(8,128)S(1)} %collective-permute-done.23.rest_1_, ...), custom_call_target="tpu_custom_call" | custom-call | tf_op jit(solution)/shard_map/pallas_call | solution.py:309
  120.5 1.5 %shard_map.66.rest_2_ = f32[1024,128]{1,0:T(8,128)S(1)} custom-call(s32[4]{0:T(128)S(1)} %copy-done.11, bf16[2,8,256,256]{3,2,1,0:T(8,128)(2,1)S(1)} %copy-done.2, f32[1024,128]{1,0:T(8,128)S(1)} %shard_map.58.rest_4_.rest_0_, f32[1024,128]{1,0:T(8,128)S(1)} %collective-permute-done.22.rest_1_, f32[1024,128]{1,0:T(8,128)S(1)} %shard_map.65.rest_2_.rest_0_), custom_call_target="tpu_custom_call" | custom-call | tf_op jit(solution)/shard_map/pallas_call | solution.py:309
  122.0 1.5 %shard_map.67.rest_4_.rest_3_ = f32[1024,128]{1,0:T(8,128)S(1)} custom-call(s32[4]{0:T(128)S(1)} %copy-done.11, bf16[2,8,256,256]{3,2,1,0:T(8,128)(2,1)S(1)} %copy-done.2, f32[1024,128]{1,0:T(8,128)S(1)} %shard_map.62.rest_0_, f32[1024,128]{1,0:T(8,128)S(1)} %collective-permute-done.21.rest_1_, f32[1024,128]{1,0:T(8,128)S(1)} %shard_map.66.rest_2_), custom_call_target="tpu_custom_call" | custom-call | tf_op jit(solution)/shard_map/pallas_call | solution.py:309
  123.5 2.2 %collective-permute-done.19.rest_2_ = f32[2,256,128]{2,1,0:T(8,128)S(1)} collective-permute-done((f32[2,256,128]{2,1,0:T(8,128)S(1)}, f32[2,256,128]{2,1,0:T(8,128)S(1)}, u32[]{:S(2)}, u32[]{:S(2)}) %collective-permute-start.19) | collective-permute-done | bytes 262176 | tf_op jit(solution)/shard_map/ppermute | solution.py:25
  125.7 4.7 %collective-permute-done.20.rest_3_ = f32[2,256,128]{2,1,0:T(8,128)S(1)} collective-permute-done((f32[2,256,128]{2,1,0:T(8,128)S(1)}, f32[2,256,128]{2,1,0:T(8,128)S(1)}, u32[]{:S(2)}, u32[]{:S(2)}) %collective-permute-start.20) | collective-permute-done | bytes 262176 | tf_op jit(solution)/shard_map/ppermute | solution.py:25
  130.4 1.5 %shard_map.68.rest_2_.rest_0_ = f32[1024,128]{1,0:T(8,128)S(1)} custom-call(s32[4]{0:T(128)S(1)} %copy-done.11, bf16[2,8,256,256]{3,2,1,0:T(8,128)(2,1)S(1)} %copy-done.4, f32[2,256,128]{2,1,0:T(8,128)S(1)} %get-tuple-element.44.rest_4_.rest_0_, f32[2,256,128]{2,1,0:T(8,128)S(1)} %collective-permute-done.18.rest_1_, ...), custom_call_target="tpu_custom_call" | custom-call | tf_op jit(solution)/shard_map/pallas_call | solution.py:309
  132.3 1.5 %shard_map.69.rest_4_.rest_5_ = f32[1024,128]{1,0:T(8,128)S(1)} custom-call(s32[4]{0:T(128)S(1)} %copy-done.11, bf16[2,8,256,256]{3,2,1,0:T(8,128)(2,1)S(1)} %copy-done.2, f32[1024,128]{1,0:T(8,128)S(1)} %shard_map.65.rest_2_.rest_0_, f32[1024,128]{1,0:T(8,128)S(1)} %collective-permute-done.26.rest_1_, f32[1024,128]{1,0:T(8,128)S(1)} %shard_map.68.rest_2_.rest_0_), custom_call_target="tpu_custom_call" | custom-call | tf_op jit(solution)/shard_map/pallas_call | solution.py:309
  133.9 2.6 %shard_map.70 = f32[8,128,512]{2,1,0:T(8,128)} custom-call(s32[4]{0:T(128)S(1)} %copy-done.11, bf16[2,8,256,256]{3,2,1,0:T(8,128)(2,1)S(1)} %copy-done.2, f32[1024,128]{1,0:T(8,128)S(1)} %shard_map.68.rest_2_.rest_0_, f32[1024,128]{1,0:T(8,128)S(1)} %collective-permute-done.25.rest_1_, f32[1024,128]{1,0:T(8,128)S(1)} %shard_map.66.rest_2_, ...), custom_call_target="tpu_custom_call" | custom-call | tf_op jit(solution)/shard_map/pallas_call | solution.py:309
  (58 shorter events, 3.1 us)
Async XLA Ops:
  3.3 39.9 %collective-permute-start.1 = (f32[1032,128]{1,0:T(8,128)}, f32[1032,128]{1,0:T(8,128)}, u32[]{:S(2)}, u32[]{:S(2)}) collective-permute-start(f32[1032,128]{1,0:T(8,128)} %shard_map.46.rest_0_.own), channel_id=1, source_target_pairs={{0,16},{4,20},{8,24},{12,28},{16,0},{20,4},{24,8},{28,12},{1,17},{... | collective-permute-start | bytes 1585160 | tf_op jit(solution)/shard_map/ppermute | solution.py:25
  11.9 54.0 %collective-permute-start = (f32[1032,128]{1,0:T(8,128)}, f32[1032,128]{1,0:T(8,128)}, u32[]{:S(2)}, u32[]{:S(2)}) collective-permute-start(f32[1032,128]{1,0:T(8,128)} %get-tuple-element.26.rest_0_.own), channel_id=1, source_target_pairs={{0,16},{4,20},{8,24},{12,28},{16,0},{20,4},{24,8},{28,12},{1,17},{... | collective-permute-start | bytes 1585160 | tf_op jit(solution)/shard_map/ppermute | solution.py:25
  12.0 3.4 %copy-start = (f32[8,8,128,256]{3,2,1,0:T(8,128)S(1)}, f32[8,8,128,256]{3,2,1,0:T(8,128)}, u32[]{:S(2)}) copy-start(f32[8,8,128,256]{3,2,1,0:T(8,128)} %g_hbm.5) | copy-start | bytes 25165828
  15.4 1.0 copy-start.8
  16.4 4.3 %copy-start.12 = (s32[1024]{0:T(1024)S(1)}, s32[1024]{0:T(1024)}, u32[]{:S(2)}) copy-start(s32[1024]{0:T(1024)} %param.7) | copy-start | bytes 12292
  18.1 1.3 copy-start.1
  19.4 1.3 copy-start.3
  21.8 1.0 copy-start.10
  22.8 20.4 %copy-start.5 = (f32[1032,128]{1,0:T(8,128)S(1)}, f32[1032,128]{1,0:T(8,128)}, u32[]{:S(2)}) copy-start(f32[1032,128]{1,0:T(8,128)} %shard_map.46.rest_0_.own) | copy-start | bytes 1585156
  22.8 20.4 %copy-start.11 = (s32[4]{0:T(128)S(1)}, s32[4]{0:T(128)}, u32[]{:S(2)}) copy-start(s32[4]{0:T(128)} %bits.27) | copy-start | bytes 52
  23.2 24.1 %copy-start.7 = (f32[1032,128]{1,0:T(8,128)S(1)}, f32[1032,128]{1,0:T(8,128)}, u32[]{:S(2)}) copy-start(f32[1032,128]{1,0:T(8,128)} %get-tuple-element.32.__0_) | copy-start | bytes 1585156
  45.3 20.6 %copy-start.6 = (f32[1032,128]{1,0:T(8,128)S(1)}, f32[1032,128]{1,0:T(8,128)}, u32[]{:S(2)}) copy-start(f32[1032,128]{1,0:T(8,128)} %get-tuple-element.31.__0_) | copy-start | bytes 1585156
  45.3 20.6 %copy-start.9 = (f32[1032,128]{1,0:T(8,128)S(1)}, f32[1032,128]{1,0:T(8,128)}, u32[]{:S(2)}) copy-start(f32[1032,128]{1,0:T(8,128)} %get-tuple-element.26.rest_0_.own) | copy-start | bytes 1585156
  45.3 22.6 %collective-permute-start.4 = (f32[512,128]{1,0:T(8,128)S(1)}, f32[512,128]{1,0:T(8,128)S(1)}, u32[]{:S(2)}, u32[]{:S(2)}) collective-permute-start(f32[512,128]{1,0:T(8,128)S(1)} %get-tuple-element.33.__2_.rest_0_), channel_id=1, source_target_pairs={{0,4},{4,0},{8,12},{12,8},{16,20},{20,16},{24,28},{28,24},{1,5},{5... | collective-permute-start | bytes 786440 | tf_op jit(solution)/shard_map/ppermute | solution.py:25
  47.2 20.7 %collective-permute-start.5 = (f32[512,128]{1,0:T(8,128)S(1)}, f32[512,128]{1,0:T(8,128)S(1)}, u32[]{:S(2)}, u32[]{:S(2)}) collective-permute-start(f32[512,128]{1,0:T(8,128)S(1)} %get-tuple-element.34.rest_1_), channel_id=1, source_target_pairs={{0,4},{4,0},{8,12},{12,8},{16,20},{20,16},{24,28},{28,24},{1,5},{5... | collective-permute-start | bytes 786440 | tf_op jit(solution)/shard_map/ppermute | solution.py:25
  47.4 28.9 %collective-permute-start.3 = (f32[1032,128]{1,0:T(8,128)S(1)}, f32[1032,128]{1,0:T(8,128)S(1)}, u32[]{:S(2)}, u32[]{:S(2)}) collective-permute-start(f32[1032,128]{1,0:T(8,128)S(1)} %shard_map.51.__2_.own), channel_id=1, source_target_pairs={{0,16},{4,20},{8,24},{12,28},{16,0},{20,4},{24,8},{28,12},{1,17},{... | collective-permute-start | bytes 1585160 | tf_op jit(solution)/shard_map/ppermute | solution.py:25
  68.9 16.8 %collective-permute-start.9 = (f32[2,2,256,128]{3,2,1,0:T(8,128)S(1)}, f32[2,2,256,128]{3,2,1,0:T(8,128)S(1)}, u32[]{:S(2)}, u32[]{:S(2)}) collective-permute-start(f32[2,2,256,128]{3,2,1,0:T(8,128)S(1)} %get-tuple-element.36.rest_0_), channel_id=1, source_target_pairs={{0,2},{1,3},{2,0},{3,1},{4,6},{5,7},{6,4},{7,5},{8,10},{9,11},{10,... | collective-permute-start | bytes 1572872 | tf_op jit(solution)/shard_map/ppermute | solution.py:25
  70.8 8.6 %collective-permute-start.10 = (f32[512,128]{1,0:T(8,128)S(1)}, f32[512,128]{1,0:T(8,128)S(1)}, u32[]{:S(2)}, u32[]{:S(2)}) collective-permute-start(f32[512,128]{1,0:T(8,128)S(1)} %get-tuple-element.35.rest_4_.rest_0_), channel_id=1, source_target_pairs={{0,4},{4,0},{8,12},{12,8},{16,20},{20,16},{24,28},{28,24},{1,5},{5... | collective-permute-start | bytes 786440 | tf_op jit(solution)/shard_map/ppermute | solution.py:25
  72.4 12.3 %collective-permute-start.11 = (f32[512,128]{1,0:T(8,128)S(1)}, f32[512,128]{1,0:T(8,128)S(1)}, u32[]{:S(2)}, u32[]{:S(2)}) collective-permute-start(f32[512,128]{1,0:T(8,128)S(1)} %get-tuple-element.40.rest_1_), channel_id=1, source_target_pairs={{0,4},{4,0},{8,12},{12,8},{16,20},{20,16},{24,28},{28,24},{1,5},{5... | collective-permute-start | bytes 786440 | tf_op jit(solution)/shard_map/ppermute | solution.py:25
  72.9 13.4 %collective-permute-start.8 = (f32[2,256,128]{2,1,0:T(8,128)S(1)}, f32[2,256,128]{2,1,0:T(8,128)S(1)}, u32[]{:S(2)}, u32[]{:S(2)}) collective-permute-start(f32[2,256,128]{2,1,0:T(8,128)S(1)} %get-tuple-element.39), channel_id=1, source_target_pairs={{0,1},{1,0},{2,3},{3,2},{4,5},{5,4},{6,7},{7,6},{8,9},{9,8},{10,11... | collective-permute-start | bytes 786440 | tf_op jit(solution)/shard_map/ppermute | solution.py:25
  76.3 25.4 %collective-permute-start.2 = (f32[1032,128]{1,0:T(8,128)S(1)}, f32[1032,128]{1,0:T(8,128)S(1)}, u32[]{:S(2)}, u32[]{:S(2)}) collective-permute-start(f32[1032,128]{1,0:T(8,128)S(1)} %shard_map.52.rest_0_.own), channel_id=1, source_target_pairs={{0,16},{4,20},{8,24},{12,28},{16,0},{20,4},{24,8},{28,12},{1,17},{... | collective-permute-start | bytes 1585160 | tf_op jit(solution)/shard_map/ppermute | solution.py:25
  79.4 8.3 %copy-start.4 = (bf16[2,8,256,256]{3,2,1,0:T(8,128)(2,1)S(1)}, bf16[2,8,256,256]{3,2,1,0:T(8,128)(2,1)}, u32[]{:S(2)}) copy-start(bf16[2,8,256,256]{3,2,1,0:T(8,128)(2,1)} %copy-done.3) | copy-start | bytes 6291460
  79.5 9.8 %collective-permute-start.6 = (f32[512,128]{1,0:T(8,128)S(1)}, f32[512,128]{1,0:T(8,128)S(1)}, u32[]{:S(2)}, u32[]{:S(2)}) collective-permute-start(f32[512,128]{1,0:T(8,128)S(1)} %get-tuple-element.37.rest_4_.rest_0_), channel_id=1, source_target_pairs={{0,4},{4,0},{8,12},{12,8},{16,20},{20,16},{24,28},{28,24},{1,5},{5... | collective-permute-start | bytes 786440 | tf_op jit(solution)/shard_map/ppermute | solution.py:25
  85.8 2.0 %collective-permute-start.12 = (f32[2,256,128]{2,1,0:T(8,128)S(1)}, f32[2,256,128]{2,1,0:T(8,128)S(1)}, u32[]{:S(2)}, u32[]{:S(2)}) collective-permute-start(f32[2,256,128]{2,1,0:T(8,128)S(1)} %shard_map.57.rest_4_), channel_id=1, source_target_pairs={{0,1},{1,0},{2,3},{3,2},{4,5},{5,4},{6,7},{7,6},{8,9},{9,8},{10,11... | collective-permute-start | bytes 786440 | tf_op jit(solution)/shard_map/ppermute | solution.py:25
  85.8 18.7 %collective-permute-start.16 = (f32[2,2,256,128]{3,2,1,0:T(8,128)S(1)}, f32[2,2,256,128]{3,2,1,0:T(8,128)S(1)}, u32[]{:S(2)}, u32[]{:S(2)}) collective-permute-start(f32[2,2,256,128]{3,2,1,0:T(8,128)S(1)} %get-tuple-element.41.rest_0_), channel_id=1, source_target_pairs={{0,2},{1,3},{2,0},{3,1},{4,6},{5,7},{6,4},{7,5},{8,10},{9,11},{10,... | collective-permute-start | bytes 1572872 | tf_op jit(solution)/shard_map/ppermute | solution.py:25
  86.2 8.4 %collective-permute-start.7 = (f32[512,128]{1,0:T(8,128)S(1)}, f32[512,128]{1,0:T(8,128)S(1)}, u32[]{:S(2)}, u32[]{:S(2)}) collective-permute-start(f32[512,128]{1,0:T(8,128)S(1)} %get-tuple-element.38.rest_1_), channel_id=1, source_target_pairs={{0,4},{4,0},{8,12},{12,8},{16,20},{20,16},{24,28},{28,24},{1,5},{5... | collective-permute-start | bytes 786440 | tf_op jit(solution)/shard_map/ppermute | solution.py:25
  95.6 15.8 %collective-permute-start.14 = (f32[2,2,256,128]{3,2,1,0:T(8,128)S(1)}, f32[2,2,256,128]{3,2,1,0:T(8,128)S(1)}, u32[]{:S(2)}, u32[]{:S(2)}) collective-permute-start(f32[2,2,256,128]{3,2,1,0:T(8,128)S(1)} %get-tuple-element.42.rest_0_), channel_id=1, source_target_pairs={{0,2},{1,3},{2,0},{3,1},{4,6},{5,7},{6,4},{7,5},{8,10},{9,11},{10,... | collective-permute-start | bytes 1572872 | tf_op jit(solution)/shard_map/ppermute | solution.py:25
  97.4 7.7 %collective-permute-start.15 = (f32[2,256,128]{2,1,0:T(8,128)S(1)}, f32[2,256,128]{2,1,0:T(8,128)S(1)}, u32[]{:S(2)}, u32[]{:S(2)}) collective-permute-start(f32[2,256,128]{2,1,0:T(8,128)S(1)} %get-tuple-element.43), channel_id=1, source_target_pairs={{0,1},{1,0},{2,3},{3,2},{4,5},{5,4},{6,7},{7,6},{8,9},{9,8},{10,11... | collective-permute-start | bytes 786440 | tf_op jit(solution)/shard_map/ppermute | solution.py:25
  103.2 12.3 %collective-permute-start.13 = (f32[1024,128]{1,0:T(8,128)S(1)}, f32[1024,128]{1,0:T(8,128)S(1)}, u32[]{:S(2)}, u32[]{:S(2)}) collective-permute-start(f32[1024,128]{1,0:T(8,128)S(1)} %shard_map.60.rest_0_), channel_id=1, source_target_pairs={{0,4},{4,0},{8,12},{12,8},{16,20},{20,16},{24,28},{28,24},{1,5},{5... | collective-permute-start | bytes 1572872 | tf_op jit(solution)/shard_map/ppermute | solution.py:25
  104.5 1.6 %collective-permute-start.17 = (f32[2,256,128]{2,1,0:T(8,128)S(1)}, f32[2,256,128]{2,1,0:T(8,128)S(1)}, u32[]{:S(2)}, u32[]{:S(2)}) collective-permute-start(f32[2,256,128]{2,1,0:T(8,128)S(1)} %shard_map.61.rest_4_), channel_id=1, source_target_pairs={{0,1},{1,0},{2,3},{3,2},{4,5},{5,4},{6,7},{7,6},{8,9},{9,8},{10,11... | collective-permute-start | bytes 786440 | tf_op jit(solution)/shard_map/ppermute | solution.py:25
  104.6 15.5 %collective-permute-start.22 = (f32[1024,128]{1,0:T(8,128)S(1)}, f32[1024,128]{1,0:T(8,128)S(1)}, u32[]{:S(2)}, u32[]{:S(2)}) collective-permute-start(f32[1024,128]{1,0:T(8,128)S(1)} %shard_map.58.rest_4_.rest_0_), channel_id=1, source_target_pairs={{0,1},{1,0},{2,3},{3,2},{4,5},{5,4},{6,7},{7,6},{8,9},{9,8},{10,11... | collective-permute-start | bytes 1572872 | tf_op jit(solution)/shard_map/ppermute | solution.py:25
  105.1 11.4 %collective-permute-start.23 = (f32[2,256,128]{2,1,0:T(8,128)S(1)}, f32[2,256,128]{2,1,0:T(8,128)S(1)}, u32[]{:S(2)}, u32[]{:S(2)}) collective-permute-start(f32[2,256,128]{2,1,0:T(8,128)S(1)} %get-tuple-element.46), channel_id=1, source_target_pairs={{0,1},{1,0},{2,3},{3,2},{4,5},{5,4},{6,7},{7,6},{8,9},{9,8},{10,11... | collective-permute-start | bytes 786440 | tf_op jit(solution)/shard_map/ppermute | solution.py:25
  107.6 14.4 %collective-permute-start.21 = (f32[1024,128]{1,0:T(8,128)S(1)}, f32[1024,128]{1,0:T(8,128)S(1)}, u32[]{:S(2)}, u32[]{:S(2)}) collective-permute-start(f32[1024,128]{1,0:T(8,128)S(1)} %shard_map.62.rest_0_), channel_id=1, source_target_pairs={{0,1},{1,0},{2,3},{3,2},{4,5},{5,4},{6,7},{7,6},{8,9},{9,8},{10,11... | collective-permute-start | bytes 1572872 | tf_op jit(solution)/shard_map/ppermute | solution.py:25
  111.4 6.1 %collective-permute-start.24 = (f32[2,256,128]{2,1,0:T(8,128)S(1)}, f32[2,256,128]{2,1,0:T(8,128)S(1)}, u32[]{:S(2)}, u32[]{:S(2)}) collective-permute-start(f32[2,256,128]{2,1,0:T(8,128)S(1)} %shard_map.63.rest_2_), channel_id=1, source_target_pairs={{0,1},{1,0},{2,3},{3,2},{4,5},{5,4},{6,7},{7,6},{8,9},{9,8},{10,11... | collective-permute-start | bytes 786440 | tf_op jit(solution)/shard_map/ppermute | solution.py:25
  116.5 7.1 %collective-permute-start.18 = (f32[2,256,128]{2,1,0:T(8,128)S(1)}, f32[2,256,128]{2,1,0:T(8,128)S(1)}, u32[]{:S(2)}, u32[]{:S(2)}) collective-permute-start(f32[2,256,128]{2,1,0:T(8,128)S(1)} %get-tuple-element.45), channel_id=1, source_target_pairs={{0,1},{1,0},{2,3},{3,2},{4,5},{5,4},{6,7},{7,6},{8,9},{9,8},{10,11... | collective-permute-start | bytes 786440 | tf_op jit(solution)/shard_map/ppermute | solution.py:25
  116.5 4.0 %copy-start.2 = (bf16[2,8,256,256]{3,2,1,0:T(8,128)(2,1)S(1)}, bf16[2,8,256,256]{3,2,1,0:T(8,128)(2,1)}, u32[]{:S(2)}) copy-start(bf16[2,8,256,256]{3,2,1,0:T(8,128)(2,1)} %copy-done.1) | copy-start | bytes 6291460
  116.6 9.2 %collective-permute-start.19 = (f32[2,256,128]{2,1,0:T(8,128)S(1)}, f32[2,256,128]{2,1,0:T(8,128)S(1)}, u32[]{:S(2)}, u32[]{:S(2)}) collective-permute-start(f32[2,256,128]{2,1,0:T(8,128)S(1)} %get-tuple-element.44.rest_4_.rest_0_), channel_id=1, source_target_pairs={{0,2},{1,3},{2,0},{3,1},{4,6},{5,7},{6,4},{7,5},{8,10},{9,11},{10,... | collective-permute-start | bytes 786440 | tf_op jit(solution)/shard_map/ppermute | solution.py:25
  117.6 12.8 %collective-permute-start.20 = (f32[2,256,128]{2,1,0:T(8,128)S(1)}, f32[2,256,128]{2,1,0:T(8,128)S(1)}, u32[]{:S(2)}, u32[]{:S(2)}) collective-permute-start(f32[2,256,128]{2,1,0:T(8,128)S(1)} %get-tuple-element.45), channel_id=1, source_target_pairs={{0,3},{1,2},{2,1},{3,0},{4,7},{5,6},{6,5},{7,4},{8,11},{9,10},{10,... | collective-permute-start | bytes 786440 | tf_op jit(solution)/shard_map/ppermute | solution.py:25
  120.1 12.2 %collective-permute-start.26 = (f32[1024,128]{1,0:T(8,128)S(1)}, f32[1024,128]{1,0:T(8,128)S(1)}, u32[]{:S(2)}, u32[]{:S(2)}) collective-permute-start(f32[1024,128]{1,0:T(8,128)S(1)} %shard_map.65.rest_2_.rest_0_), channel_id=1, source_target_pairs={{0,1},{1,0},{2,3},{3,2},{4,5},{5,4},{6,7},{7,6},{8,9},{9,8},{10,11... | collective-permute-start | bytes 1572872 | tf_op jit(solution)/shard_map/ppermute | solution.py:25
  131.9 2.0 %collective-permute-start.25 = (f32[1024,128]{1,0:T(8,128)S(1)}, f32[1024,128]{1,0:T(8,128)S(1)}, u32[]{:S(2)}, u32[]{:S(2)}) collective-permute-start(f32[1024,128]{1,0:T(8,128)S(1)} %shard_map.68.rest_2_.rest_0_), channel_id=1, source_target_pairs={{0,1},{1,0},{2,3},{3,2},{4,5},{5,4},{6,7},{7,6},{8,9},{9,8},{10,11... | collective-permute-start | bytes 1572872 | tf_op jit(solution)/shard_map/ppermute | solution.py:25

commit v2 on v1

--- a/solution.py
+++ b/solution.py
@@ -15,7 +15,7 @@
 LAG = (0, 2, 2, 2)
 CORE_SPLIT = 1
 Y_CUTS = (2, 2, 2, 1)
-JOINT = 3
+JOINT = (1, 1, 1, 0)
 STAGES = (1, 3, 4, 6)
 VMEM_LIMIT = 16 * 1024 * 1024
 FIRST_LIMIT = 62 * 1024 * 1024
@@ -110,6 +110,7 @@
         top = jnp.concatenate([g_ref[low], g_ref[high]], axis=0)
         return jnp.concatenate(split2(top), axis=0)
 
+    bit = bits(0)
     for (group, part, parts), out_ref in zip(chunks, outs):
         width = lanes // parts
         begin = (group - first) * lanes + part * width
@@ -121,7 +122,7 @@
             else:
                 after[span, :width] = value
 
-        local_level(state, rank, blocks, bits[0], put, slice(begin, begin + width))
+        local_level(state, rank, blocks, bit, put, slice(begin, begin + width))
         if parts > 1:
             out_ref[:run, :] = jnp.concatenate(
                 [after[at * run:(at + 1) * run, :width] for at in range(parts)], axis=1
@@ -187,6 +188,21 @@
         put(node * rank, rank, value)
 
 
+def with_bits(kernel):
+    def body(bits_hbm, *refs):
+        *refs, bits_ref, arrived = refs
+        copy = pltpu.make_async_copy(bits_hbm, bits_ref, arrived)
+        copy.start()
+
+        def bits(slot):
+            copy.wait()
+            return bits_ref[slot]
+
+        kernel(bits, *refs)
+
+    return body
+
+
 def put_rows(ref):
     def put(first, count, value):
         ref[first:first + count, :] = value
@@ -201,7 +217,7 @@
         lambda first, count: unpack([own], first, count, parts, PAD),
         lambda first, count: unpack([other], first, count, parts, PAD),
     )
-    packed_level(before, blocks, level + 1, bits[slot], outs, after, parts)
+    packed_level(before, blocks, level + 1, bits(slot), outs, after, parts)
 
 
 def last_kernel(parts, part, done, axis, shift, level, slot, bits, blocks, *rest):
@@ -231,7 +247,7 @@
     def put(span, value):
         target[span, part * width:(part + 1) * width] = value
 
-    local_level(before, rank, split_blocks(blocks, level + 1), bits[slot], put)
+    local_level(before, rank, split_blocks(blocks, level + 1), bits(slot), put)
     for copy in copies[-1:]:
         copy.start()
     for copy in copies:
@@ -285,10 +301,9 @@
         before[span] = product(
             blocks[level, node], jnp.concatenate([both[0, span], both[1, span]], axis=0)
         )
-    packed_level(before, blocks, level + 1, bits[slot], outs, after, parts)
-
-
-SMEM = pl.BlockSpec(memory_space=pltpu.SMEM)
+    packed_level(before, blocks, level + 1, bits(slot), outs, after, parts)
+
+
 VMEM = pl.BlockSpec(memory_space=pltpu.VMEM)
 HBM = pl.BlockSpec(memory_space=pltpu.HBM)
 ANY = pl.BlockSpec(memory_space=pl.ANY)
@@ -306,6 +321,9 @@
 
     def run(kernel, out_shape, in_specs, out_specs, scratch, args, aliases=None, limit=VMEM_LIMIT):
         extra = [store["token"]] if "token" in store else []
+        if args[0] is local_bits:
+            kernel = with_bits(kernel)
+            scratch = [*scratch, pltpu.SMEM(local_bits.shape, jnp.int32), pltpu.SemaphoreType.DMA]
         out = pl.pallas_call(
             kernel,
             out_shape=out_shape,
@@ -331,7 +349,7 @@
         out = run(
             functools.partial(first_kernel, tuple(wanted)),
             [shape((rows // parts + PAD, GROUP), F32) for _, _, parts in wanted],
-            [SMEM, HBM, HBM],
+            [HBM, HBM, HBM],
             [VMEM] * len(wanted),
             [
                 pltpu.VMEM((nodes, rank, groups * GROUP), F32),
@@ -391,7 +409,7 @@
         own = run(
             functools.partial(pair_kernel, parts, cuts, "src", src_far.bit_length() - 1, 0, 1),
             packed(parts, cuts),
-            [SMEM, VMEM, VMEM, VMEM] + [ANY] * len(ended),
+            [HBM, VMEM, VMEM, VMEM] + [ANY] * len(ended),
             [VMEM] * cuts,
             narrow(parts, 2),
             [local_bits, store["blocks", 1], store["whole", index], store["far", index], *ended],
@@ -402,10 +420,10 @@
     def step_c(index):
         _, _, parts = chunks[index]
         cuts = Y_CUTS[index]
-        joint = index < JOINT
+        joint = JOINT[index]
         piece = (2, rows // n_tgt // parts, GROUP)
         pieces = run(
-            functools.partial(relabel_kernel, parts, cuts, tgt_far, joint, "src", 0, 0),
+            functools.partial(relabel_kernel, parts, cuts, tgt_far, bool(joint), "src", 0, 0),
             [shape((tgt_far, 2, piece[1] + PAD_X, GROUP), F32), shape(piece, F32)] if joint else [shape(piece, F32)] * tgt_far,
             [VMEM] * (2 + 2 * cuts),
             [VMEM] * (2 if joint else tgt_far),
@@ -419,7 +437,7 @@
         store["moved", index, 1] = partner_2(store["piece", index, 1 % tgt_far], "tgt", 1)
 
     def step_x(index):
-        if index >= JOINT:
+        if not JOINT[index]:
             for offset in range(2, n_tgt):
                 store["moved", index, offset] = partner_2(
                     store["piece", index, offset % tgt_far], "tgt", offset
@@ -432,7 +450,7 @@
             store["moved", index, offset] = partner_2(both, "tgt", offset)
 
     def step_s(index):
-        if index < JOINT:
+        if JOINT[index]:
             for offset in range(2, n_tgt, 2):
                 joint = store["moved", index, offset]
                 cross = run(cross_kernel, [shape(joint.shape[1:], F32)], [VMEM], [VMEM], [], [joint])[0]
@@ -440,12 +458,12 @@
 
     def step_d(index):
         _, _, parts = chunks[index]
-        joint = index < JOINT
+        joint = JOINT[index]
         picks = tuple(0 if joint and offset % 2 == 0 else None for offset in range(n_tgt))
         store["mid", index] = run(
             functools.partial(gather_kernel, parts, n_tgt, picks, "tgt", 0, 2),
             packed(parts, CORE_SPLIT),
-            [SMEM, VMEM] + [VMEM] * n_tgt,
+            [HBM, VMEM] + [VMEM] * n_tgt,
             [VMEM] * CORE_SPLIT,
             [pltpu.VMEM((2, rows, GROUP // parts), F32)] + narrow(parts, 2),
             [
@@ -464,7 +482,7 @@
         store["out", index] = run(
             functools.partial(last_kernel, parts, part, len(CUTS) - 1 if final else 0, "tgt", 0, 0, 3),
             [shape((nodes, rank, columns) if final else (rows, GROUP), F32)],
-            [SMEM, VMEM] + [VMEM] * (2 * CORE_SPLIT + len(earlier)),
+            [HBM, VMEM] + [VMEM] * (2 * CORE_SPLIT + len(earlier)),
             [HBM if final else VMEM],
             narrow(parts, 1) + [pltpu.VMEM((rows, GROUP), F32), pltpu.SemaphoreType.DMA((len(CUTS),))],
             [local_bits, store["blocks", 6], *store["mid", index], *store["core", index], *earlier],
@@ -475,35 +493,8 @@
         "B": step_b, "C": step_c, "T": step_t, "X": step_x, "S": step_s, "D": step_d, "E": step_e,
     }
 
-    def follow(names):
-        for name in names:
-            steps[name[0]](int(name[1:]))
-
-    kept = ("piece", "moved", "out")
-
-    def apart(names):
-        def work():
-            before = dict(store)
-            follow(names)
-            made = {key: value for key, value in store.items() if before.get(key) is not value and key[0] in kept}
-            keys.extend(key for key in made if key not in keys)
-            store.clear()
-            store.update(before)
-            return list(made.values())
-
-        keys = []
-        shapes = jax.eval_shape(work)
-        made = lax.cond(
-            local_bits[0] >= 0, work, lambda: jax.tree.map(lambda x: jnp.zeros(x.shape, x.dtype), shapes)
-        )
-        store.update(zip(keys, made))
-        store["token"] = made[0]
-
-    for names in ORDER:
-        if isinstance(names, str):
-            follow([names])
-        else:
-            apart(names)
+    for name in ORDER:
+        steps[name[0]](int(name[1:]))
     return store["out", len(chunks) - 1]
 
 

time: 137 us -> 135 us (0.985)
  Pallas kernels: 34.2 us -> 29.1 us
  waiting for transfers between devices: 72.4 us -> 75.5 us
    pallas_call x25, Pallas kernels: 34.2 us -> 29.1 us  [run(): pl.pallas_call(kernel, out_shape=out_shape, in_specs=list(in_specs) + [AN...]
    ppermute x27, waiting for transfers between devices: 72.4 us -> 75.5 us  [partner_2(): lax.ppermute(shard, axis, [(i, i ^ mask) for i in range(lax.axis_size(axi...]
  transfers between devices with their start and end apart: 27 -> 27, of which waited for: 13 -> 13; matrix products, arithmetic and copies ran while one was open for 1% -> 1% of each run, Pallas kernels for 21% -> 18%
where the time goes in v2:
time: 135 us
  waiting for transfers between devices  75.5 us (56%)
  Pallas kernels  29.1 us (22%)
  starting transfers between devices  20.3 us (15%)
  local copies, waits for them, and re-layouts  9.18 us (7%)
    ppermute x27, waiting for transfers between devices, partner_2(): lax.ppermute(shard, axis, [(i, i ^ mask) for i in range(lax.axis_size(axi...  75.5 us
    pallas_call x25, Pallas kernels, run(): pl.pallas_call(kernel, out_shape=out_shape, in_specs=list(in_specs) + [AN...  29.1 us
    ppermute x27, starting transfers between devices, partner_2(): lax.ppermute(shard, axis, [(i, i ^ mask) for i in range(lax.axis_size(axi...  20.3 us
    unnamed x26, local copies, waits for them, and re-layouts  8.15 us
  transfers between devices with their start and end apart: 27, of which 13 were waited for; matrix products, arithmetic and copies ran while one was open for 1% of the time, Pallas kernels for 18%

profile of v2, /device:TPU:0, one launch (start us, length us, event | category | flops | bytes accessed | tf_op | source)
XLA Modules:
  0.0 134.5 jit_solution(10795675084955533602)
XLA Ops:
  0.0 2.7 %shard_map.46.refs_2_.refs_1_ = f32[1032,128]{1,0:T(8,128)} custom-call(s32[4]{0:T(128)} %bits_hbm.27, f32[8,128,512]{2,1,0:T(8,128)} %refs_0_.3, f32[8,8,128,256]{3,2,1,0:T(8,128)} %g_hbm.1), custom_call_target="tpu_custom_call" | custom-call | tf_op jit(solution)/shard_map/pallas_call | solution.py:327
  2.7 4.1 %collective-permute-start.1 = (f32[1032,128]{1,0:T(8,128)}, f32[1032,128]{1,0:T(8,128)}, u32[]{:S(2)}, u32[]{:S(2)}) collective-permute-start(f32[1032,128]{1,0:T(8,128)} %shard_map.46.refs_2_.refs_1_), channel_id=1, source_target_pairs={{0,16},{4,20},{8,24},{12,28},{16,0},{20,4},{24,8},{28,12},{1,17},{... | collective-permute-start | bytes 1585160 | tf_op jit(solution)/shard_map/ppermute | solution.py:25
  6.8 3.8 %shard_map.47 = (f32[1032,128]{1,0:T(8,128)}, f32[1032,128]{1,0:T(8,128)}, f32[1032,128]{1,0:T(8,128)}) custom-call(s32[4]{0:T(128)} %bits_hbm.27, f32[8,128,512]{2,1,0:T(8,128)} %refs_0_.3, f32[8,8,128,256]{3,2,1,0:T(8,128)} %g_hbm.1, f32[1032,128]{1,0:T(8,128)} %shard_map.46.refs_2_.refs_1_), custom_call_target="tpu_custom_call" | custom-call | tf_op jit(solution)/shard_map/pallas_call | solution.py:327
  10.7 3.4 %copy-done = f32[8,8,128,256]{3,2,1,0:T(8,128)S(1)} copy-done((f32[8,8,128,256]{3,2,1,0:T(8,128)S(1)}, f32[8,8,128,256]{3,2,1,0:T(8,128)}, u32[]{:S(2)}) %copy-start) | copy-done | bytes 8388632
  14.1 1.0 copy-done.8
  15.1 1.6 %shard_map.48 = (bf16[2,8,256,256]{3,2,1,0:T(8,128)(2,1)S(1)}, bf16[1,8,256,256]{3,2,1,0:T(8,128)(2,1)S(1)}, bf16[2,8,256,256]{3,2,1,0:T(8,128)(2,1)S(1)}, bf16[2,8,256,256]{3,2,1,0:T(8,128)(2,1)S(1)}) custom-call(f32[8,8,128,256]{3,2,1,0:T(8,128)S(1)} %copy-done, f32[1032,128]{1,0:T(8,128)S(1)} %copy-done.8), custom_call_target="tpu_custom_call" | custom-call | tf_op jit(solution)/shard_map/pallas_call | solution.py:327
  16.8 1.3 copy-done.1
  18.1 1.3 copy-done.3
  19.4 1.0 copy.7.relabel_ref
  20.5 1.0 copy-done.10
  21.9 20.7 %collective-permute-done.1.refs_2_.__1_ = f32[1032,128]{1,0:T(8,128)} collective-permute-done((f32[1032,128]{1,0:T(8,128)}, f32[1032,128]{1,0:T(8,128)}, u32[]{:S(2)}, u32[]{:S(2)}) %collective-permute-start.1) | collective-permute-done | bytes 528416 | tf_op jit(solution)/shard_map/ppermute | solution.py:25
  42.6 2.1 %shard_map.50 = (f32[512,128]{1,0:T(8,128)S(1)}, f32[512,128]{1,0:T(8,128)S(1)}) custom-call(s32[4]{0:T(128)S(1)} %copy-done.11, bf16[2,8,256,256]{3,2,1,0:T(8,128)(2,1)S(1)} %get-tuple-element.30.rest_0_.refs_0_, f32[1032,128]{1,0:T(8,128)S(1)} %copy-done.5, f32[1032,128]{1,0:T(8,128)} %collective-permute-done.1.refs_2_.__1_, ...), custom_call_target="tpu_custom_call" | custom-call | tf_op jit(solution)/shard_map/pallas_call | solution.py:327
  44.7 1.9 %collective-permute-start.4 = (f32[512,128]{1,0:T(8,128)S(1)}, f32[512,128]{1,0:T(8,128)S(1)}, u32[]{:S(2)}, u32[]{:S(2)}) collective-permute-start(f32[512,128]{1,0:T(8,128)S(1)} %get-tuple-element.33.__2_.rest_0_), channel_id=1, source_target_pairs={{0,4},{4,0},{8,12},{12,8},{16,20},{20,16},{24,28},{28,24},{1,5},{5... | collective-permute-start | bytes 786440 | tf_op jit(solution)/shard_map/ppermute | solution.py:25
  46.8 18.4 %collective-permute-done.__1_.refs_2_ = f32[1032,128]{1,0:T(8,128)} collective-permute-done((f32[1032,128]{1,0:T(8,128)}, f32[1032,128]{1,0:T(8,128)}, u32[]{:S(2)}, u32[]{:S(2)}) %collective-permute-start) | collective-permute-done | bytes 528416 | tf_op jit(solution)/shard_map/ppermute | solution.py:25
  65.2 2.1 %shard_map.53 = (f32[512,128]{1,0:T(8,128)S(1)}, f32[512,128]{1,0:T(8,128)S(1)}) custom-call(s32[4]{0:T(128)S(1)} %copy-done.11, bf16[2,8,256,256]{3,2,1,0:T(8,128)(2,1)S(1)} %get-tuple-element.30.rest_0_.refs_0_, f32[1032,128]{1,0:T(8,128)S(1)} %copy-done.9, f32[1032,128]{1,0:T(8,128)} %collective-permute-done.__1_.refs_2_, ...), custom_call_target="tpu_custom_call" | custom-call | tf_op jit(solution)/shard_map/pallas_call | solution.py:327
  67.4 1.0 shard_map.54
  68.4 1.9 %collective-permute-start.9 = (f32[2,2,256,128]{3,2,1,0:T(8,128)S(1)}, f32[2,2,256,128]{3,2,1,0:T(8,128)S(1)}, u32[]{:S(2)}, u32[]{:S(2)}) collective-permute-start(f32[2,2,256,128]{3,2,1,0:T(8,128)S(1)} %get-tuple-element.36.refs_3_.refs_1_), channel_id=1, source_target_pairs={{0,2},{1,3},{2,0},{3,1},{4,6},{5,7},{6,4},{7,5},{8,10},{9,11},{10,... | collective-permute-start | bytes 1572872 | tf_op jit(solution)/shard_map/ppermute | solution.py:25
  70.3 1.5 %collective-permute-start.10 = (f32[512,128]{1,0:T(8,128)S(1)}, f32[512,128]{1,0:T(8,128)S(1)}, u32[]{:S(2)}, u32[]{:S(2)}) collective-permute-start(f32[512,128]{1,0:T(8,128)S(1)} %get-tuple-element.35.rest_4_.rest_0_), channel_id=1, source_target_pairs={{0,4},{4,0},{8,12},{12,8},{16,20},{20,16},{24,28},{28,24},{1,5},{5... | collective-permute-start | bytes 786440 | tf_op jit(solution)/shard_map/ppermute | solution.py:25
  72.3 3.3 %collective-permute-done.3.refs_2_ = f32[1032,128]{1,0:T(8,128)S(1)} collective-permute-done((f32[1032,128]{1,0:T(8,128)S(1)}, f32[1032,128]{1,0:T(8,128)S(1)}, u32[]{:S(2)}, u32[]{:S(2)}) %collective-permute-start.3) | collective-permute-done | bytes 528416 | tf_op jit(solution)/shard_map/ppermute | solution.py:25
  75.6 1.0 shard_map.55
  76.7 2.4 %collective-permute-done.10.rest_2_ = f32[512,128]{1,0:T(8,128)S(1)} collective-permute-done((f32[512,128]{1,0:T(8,128)S(1)}, f32[512,128]{1,0:T(8,128)S(1)}, u32[]{:S(2)}, u32[]{:S(2)}) %collective-permute-start.10) | collective-permute-done | bytes 262176 | tf_op jit(solution)/shard_map/ppermute | solution.py:25
  79.1 1.8 %collective-permute-start.6 = (f32[512,128]{1,0:T(8,128)S(1)}, f32[512,128]{1,0:T(8,128)S(1)}, u32[]{:S(2)}, u32[]{:S(2)}) collective-permute-start(f32[512,128]{1,0:T(8,128)S(1)} %get-tuple-element.37.rest_4_.rest_0_), channel_id=1, source_target_pairs={{0,4},{4,0},{8,12},{12,8},{16,20},{20,16},{24,28},{28,24},{1,5},{5... | collective-permute-start | bytes 786440 | tf_op jit(solution)/shard_map/ppermute | solution.py:25
  80.8 3.7 %collective-permute-done.11.rest_3_ = f32[512,128]{1,0:T(8,128)S(1)} collective-permute-done((f32[512,128]{1,0:T(8,128)S(1)}, f32[512,128]{1,0:T(8,128)S(1)}, u32[]{:S(2)}, u32[]{:S(2)}) %collective-permute-start.11) | collective-permute-done | bytes 262176 | tf_op jit(solution)/shard_map/ppermute | solution.py:25
  84.5 1.0 shard_map.56
  85.6 0.6 collective-permute-start.16
  86.2 1.1 collective-permute-start.7
  87.3 1.0 shard_map.58.rest_4_.refs_1_
  88.4 6.2 %collective-permute-done.7.rest_3_ = f32[512,128]{1,0:T(8,128)S(1)} collective-permute-done((f32[512,128]{1,0:T(8,128)S(1)}, f32[512,128]{1,0:T(8,128)S(1)}, u32[]{:S(2)}, u32[]{:S(2)}) %collective-permute-start.7) | collective-permute-done | bytes 262176 | tf_op jit(solution)/shard_map/ppermute | solution.py:25
  94.6 1.0 shard_map.59
  95.6 1.6 %collective-permute-start.14 = (f32[2,2,256,128]{3,2,1,0:T(8,128)S(1)}, f32[2,2,256,128]{3,2,1,0:T(8,128)S(1)}, u32[]{:S(2)}, u32[]{:S(2)}) collective-permute-start(f32[2,2,256,128]{3,2,1,0:T(8,128)S(1)} %get-tuple-element.42.refs_3_.refs_1_), channel_id=1, source_target_pairs={{0,2},{1,3},{2,0},{3,1},{4,6},{5,7},{6,4},{7,5},{8,10},{9,11},{10,... | collective-permute-start | bytes 1572872 | tf_op jit(solution)/shard_map/ppermute | solution.py:25
  97.2 3.8 %collective-permute-done.2.refs_2_ = f32[1032,128]{1,0:T(8,128)S(1)} collective-permute-done((f32[1032,128]{1,0:T(8,128)S(1)}, f32[1032,128]{1,0:T(8,128)S(1)}, u32[]{:S(2)}, u32[]{:S(2)}) %collective-permute-start.2) | collective-permute-done | bytes 528416 | tf_op jit(solution)/shard_map/ppermute | solution.py:25
  101.0 1.2 shard_map.60.rest_0_
  102.3 1.3 %collective-permute-start.13 = (f32[1024,128]{1,0:T(8,128)S(1)}, f32[1024,128]{1,0:T(8,128)S(1)}, u32[]{:S(2)}, u32[]{:S(2)}) collective-permute-start(f32[1024,128]{1,0:T(8,128)S(1)} %shard_map.60.rest_0_), channel_id=1, source_target_pairs={{0,4},{4,0},{8,12},{12,8},{16,20},{20,16},{24,28},{28,24},{1,5},{5... | collective-permute-start | bytes 1572872 | tf_op jit(solution)/shard_map/ppermute | solution.py:25
  104.3 0.9 collective-permute-done.17.refs_4_
  105.3 1.0 shard_map.62.rest_0_.refs_1_
  106.5 4.7 %collective-permute-done.14.joint.refs_3_ = f32[2,2,256,128]{3,2,1,0:T(8,128)S(1)} collective-permute-done((f32[2,2,256,128]{3,2,1,0:T(8,128)S(1)}, f32[2,2,256,128]{3,2,1,0:T(8,128)S(1)}, u32[]{:S(2)}, u32[]{:S(2)}) %collective-permute-start.14) | collective-permute-done | bytes 524320 | tf_op jit(solution)/shard_map/ppermute | solution.py:25
  111.3 3.2 %collective-permute-done.13.rest_1_ = f32[1024,128]{1,0:T(8,128)S(1)} collective-permute-done((f32[1024,128]{1,0:T(8,128)S(1)}, f32[1024,128]{1,0:T(8,128)S(1)}, u32[]{:S(2)}, u32[]{:S(2)}) %collective-permute-start.13) | collective-permute-done | bytes 524320 | tf_op jit(solution)/shard_map/ppermute | solution.py:25
  114.5 1.0 shard_map.64
  115.7 1.0 collective-permute-start.19
  116.7 0.8 collective-permute-start.20
  117.5 1.2 shard_map.65.refs_3_.refs_1_
  119.2 1.3 shard_map.66.refs_3_
  120.5 1.3 shard_map.67.refs_5_.refs_4_
  121.8 3.1 %collective-permute-done.19.refs_3_ = f32[2,256,128]{2,1,0:T(8,128)S(1)} collective-permute-done((f32[2,256,128]{2,1,0:T(8,128)S(1)}, f32[2,256,128]{2,1,0:T(8,128)S(1)}, u32[]{:S(2)}, u32[]{:S(2)}) %collective-permute-start.19) | collective-permute-done | bytes 262176 | tf_op jit(solution)/shard_map/ppermute | solution.py:25
  124.8 4.7 %collective-permute-done.20.refs_4_ = f32[2,256,128]{2,1,0:T(8,128)S(1)} collective-permute-done((f32[2,256,128]{2,1,0:T(8,128)S(1)}, f32[2,256,128]{2,1,0:T(8,128)S(1)}, u32[]{:S(2)}, u32[]{:S(2)}) %collective-permute-start.20) | collective-permute-done | bytes 262176 | tf_op jit(solution)/shard_map/ppermute | solution.py:25
  129.5 1.0 shard_map.68.refs_3_.refs_1_
  130.9 1.3 shard_map.69.refs_5_.refs_6_
  132.5 1.8 %shard_map.70 = f32[8,128,512]{2,1,0:T(8,128)} custom-call(s32[4]{0:T(128)S(1)} %copy-done.11, bf16[2,8,256,256]{3,2,1,0:T(8,128)(2,1)S(1)} %copy-done.2, f32[1024,128]{1,0:T(8,128)S(1)} %shard_map.68.refs_3_.refs_1_, f32[1024,128]{1,0:T(8,128)S(1)} %collective-permute-done.25.refs_2_, f32[1024,128]{1,0:T(8,128)S(1)} %shard_map.66.refs_3_, ...), custom_call_target="tpu_custom_call" | custom-call | tf_op jit(solution)/shard_map/pallas_call | solution.py:327
  (58 shorter events, 3.5 us)
Async XLA Ops:
  2.7 39.9 %collective-permute-start.1 = (f32[1032,128]{1,0:T(8,128)}, f32[1032,128]{1,0:T(8,128)}, u32[]{:S(2)}, u32[]{:S(2)}) collective-permute-start(f32[1032,128]{1,0:T(8,128)} %shard_map.46.refs_2_.refs_1_), channel_id=1, source_target_pairs={{0,16},{4,20},{8,24},{12,28},{16,0},{20,4},{24,8},{28,12},{1,17},{... | collective-permute-start | bytes 1585160 | tf_op jit(solution)/shard_map/ppermute | solution.py:25
  10.6 54.6 %collective-permute-start = (f32[1032,128]{1,0:T(8,128)}, f32[1032,128]{1,0:T(8,128)}, u32[]{:S(2)}, u32[]{:S(2)}) collective-permute-start(f32[1032,128]{1,0:T(8,128)} %get-tuple-element.26.rest_0_.refs_1_), channel_id=1, source_target_pairs={{0,16},{4,20},{8,24},{12,28},{16,0},{20,4},{24,8},{28,12},{1,17},{... | collective-permute-start | bytes 1585160 | tf_op jit(solution)/shard_map/ppermute | solution.py:25
  10.7 3.4 %copy-start = (f32[8,8,128,256]{3,2,1,0:T(8,128)S(1)}, f32[8,8,128,256]{3,2,1,0:T(8,128)}, u32[]{:S(2)}) copy-start(f32[8,8,128,256]{3,2,1,0:T(8,128)} %g_hbm.1) | copy-start | bytes 25165828
  14.1 1.0 copy-start.8
  15.1 4.3 %copy-start.12 = (s32[1024]{0:T(1024)S(1)}, s32[1024]{0:T(1024)}, u32[]{:S(2)}) copy-start(s32[1024]{0:T(1024)} %param.7) | copy-start | bytes 12292
  16.8 1.3 copy-start.1
  18.1 1.3 copy-start.3
  20.5 1.0 copy-start.10
  21.5 21.1 %copy-start.5 = (f32[1032,128]{1,0:T(8,128)S(1)}, f32[1032,128]{1,0:T(8,128)}, u32[]{:S(2)}) copy-start(f32[1032,128]{1,0:T(8,128)} %shard_map.46.refs_2_.refs_1_) | copy-start | bytes 1585156
  21.5 21.1 %copy-start.11 = (s32[4]{0:T(128)S(1)}, s32[4]{0:T(128)}, u32[]{:S(2)}) copy-start(s32[4]{0:T(128)} %bits_hbm.27) | copy-start | bytes 52
  21.9 24.9 %copy-start.7 = (f32[1032,128]{1,0:T(8,128)S(1)}, f32[1032,128]{1,0:T(8,128)}, u32[]{:S(2)}) copy-start(f32[1032,128]{1,0:T(8,128)} %get-tuple-element.32.__0_) | copy-start | bytes 1585156
  44.7 20.5 %copy-start.6 = (f32[1032,128]{1,0:T(8,128)S(1)}, f32[1032,128]{1,0:T(8,128)}, u32[]{:S(2)}) copy-start(f32[1032,128]{1,0:T(8,128)} %get-tuple-element.31.__0_) | copy-start | bytes 1585156
  44.7 20.5 %copy-start.9 = (f32[1032,128]{1,0:T(8,128)S(1)}, f32[1032,128]{1,0:T(8,128)}, u32[]{:S(2)}) copy-start(f32[1032,128]{1,0:T(8,128)} %get-tuple-element.26.rest_0_.refs_1_) | copy-start | bytes 1585156
  44.7 22.6 %collective-permute-start.4 = (f32[512,128]{1,0:T(8,128)S(1)}, f32[512,128]{1,0:T(8,128)S(1)}, u32[]{:S(2)}, u32[]{:S(2)}) collective-permute-start(f32[512,128]{1,0:T(8,128)S(1)} %get-tuple-element.33.__2_.rest_0_), channel_id=1, source_target_pairs={{0,4},{4,0},{8,12},{12,8},{16,20},{20,16},{24,28},{28,24},{1,5},{5... | collective-permute-start | bytes 786440 | tf_op jit(solution)/shard_map/ppermute | solution.py:25
  46.6 20.7 %collective-permute-start.5 = (f32[512,128]{1,0:T(8,128)S(1)}, f32[512,128]{1,0:T(8,128)S(1)}, u32[]{:S(2)}, u32[]{:S(2)}) collective-permute-start(f32[512,128]{1,0:T(8,128)S(1)} %get-tuple-element.34.rest_1_), channel_id=1, source_target_pairs={{0,4},{4,0},{8,12},{12,8},{16,20},{20,16},{24,28},{28,24},{1,5},{5... | collective-permute-start | bytes 786440 | tf_op jit(solution)/shard_map/ppermute | solution.py:25
  46.8 28.8 %collective-permute-start.3 = (f32[1032,128]{1,0:T(8,128)S(1)}, f32[1032,128]{1,0:T(8,128)S(1)}, u32[]{:S(2)}, u32[]{:S(2)}) collective-permute-start(f32[1032,128]{1,0:T(8,128)S(1)} %shard_map.51.__2_.refs_1_), channel_id=1, source_target_pairs={{0,16},{4,20},{8,24},{12,28},{16,0},{20,4},{24,8},{28,12},{1,17},{... | collective-permute-start | bytes 1585160 | tf_op jit(solution)/shard_map/ppermute | solution.py:25
  68.4 17.1 %collective-permute-start.9 = (f32[2,2,256,128]{3,2,1,0:T(8,128)S(1)}, f32[2,2,256,128]{3,2,1,0:T(8,128)S(1)}, u32[]{:S(2)}, u32[]{:S(2)}) collective-permute-start(f32[2,2,256,128]{3,2,1,0:T(8,128)S(1)} %get-tuple-element.36.refs_3_.refs_1_), channel_id=1, source_target_pairs={{0,2},{1,3},{2,0},{3,1},{4,6},{5,7},{6,4},{7,5},{8,10},{9,11},{10,... | collective-permute-start | bytes 1572872 | tf_op jit(solution)/shard_map/ppermute | solution.py:25
  70.3 8.8 %collective-permute-start.10 = (f32[512,128]{1,0:T(8,128)S(1)}, f32[512,128]{1,0:T(8,128)S(1)}, u32[]{:S(2)}, u32[]{:S(2)}) collective-permute-start(f32[512,128]{1,0:T(8,128)S(1)} %get-tuple-element.35.rest_4_.rest_0_), channel_id=1, source_target_pairs={{0,4},{4,0},{8,12},{12,8},{16,20},{20,16},{24,28},{28,24},{1,5},{5... | collective-permute-start | bytes 786440 | tf_op jit(solution)/shard_map/ppermute | solution.py:25
  71.8 12.7 %collective-permute-start.11 = (f32[512,128]{1,0:T(8,128)S(1)}, f32[512,128]{1,0:T(8,128)S(1)}, u32[]{:S(2)}, u32[]{:S(2)}) collective-permute-start(f32[512,128]{1,0:T(8,128)S(1)} %get-tuple-element.40.rest_1_), channel_id=1, source_target_pairs={{0,4},{4,0},{8,12},{12,8},{16,20},{20,16},{24,28},{28,24},{1,5},{5... | collective-permute-start | bytes 786440 | tf_op jit(solution)/shard_map/ppermute | solution.py:25
  72.3 13.9 %collective-permute-start.8 = (f32[2,256,128]{2,1,0:T(8,128)S(1)}, f32[2,256,128]{2,1,0:T(8,128)S(1)}, u32[]{:S(2)}, u32[]{:S(2)}) collective-permute-start(f32[2,256,128]{2,1,0:T(8,128)S(1)} %get-tuple-element.39), channel_id=1, source_target_pairs={{0,1},{1,0},{2,3},{3,2},{4,5},{5,4},{6,7},{7,6},{8,9},{9,8},{10,11... | collective-permute-start | bytes 786440 | tf_op jit(solution)/shard_map/ppermute | solution.py:25
  75.6 25.4 %collective-permute-start.2 = (f32[1032,128]{1,0:T(8,128)S(1)}, f32[1032,128]{1,0:T(8,128)S(1)}, u32[]{:S(2)}, u32[]{:S(2)}) collective-permute-start(f32[1032,128]{1,0:T(8,128)S(1)} %shard_map.52.refs_3_.refs_1_), channel_id=1, source_target_pairs={{0,16},{4,20},{8,24},{12,28},{16,0},{20,4},{24,8},{28,12},{1,17},{... | collective-permute-start | bytes 1585160 | tf_op jit(solution)/shard_map/ppermute | solution.py:25
  79.1 8.2 %copy-start.4 = (bf16[2,8,256,256]{3,2,1,0:T(8,128)(2,1)S(1)}, bf16[2,8,256,256]{3,2,1,0:T(8,128)(2,1)}, u32[]{:S(2)}) copy-start(bf16[2,8,256,256]{3,2,1,0:T(8,128)(2,1)} %copy-done.3) | copy-start | bytes 6291460
  79.1 9.3 %collective-permute-start.6 = (f32[512,128]{1,0:T(8,128)S(1)}, f32[512,128]{1,0:T(8,128)S(1)}, u32[]{:S(2)}, u32[]{:S(2)}) collective-permute-start(f32[512,128]{1,0:T(8,128)S(1)} %get-tuple-element.37.rest_4_.rest_0_), channel_id=1, source_target_pairs={{0,4},{4,0},{8,12},{12,8},{16,20},{20,16},{24,28},{28,24},{1,5},{5... | collective-permute-start | bytes 786440 | tf_op jit(solution)/shard_map/ppermute | solution.py:25
  85.6 1.8 %collective-permute-start.12 = (f32[2,256,128]{2,1,0:T(8,128)S(1)}, f32[2,256,128]{2,1,0:T(8,128)S(1)}, u32[]{:S(2)}, u32[]{:S(2)}) collective-permute-start(f32[2,256,128]{2,1,0:T(8,128)S(1)} %shard_map.57.refs_5_), channel_id=1, source_target_pairs={{0,1},{1,0},{2,3},{3,2},{4,5},{5,4},{6,7},{7,6},{8,9},{9,8},{10,11... | collective-permute-start | bytes 786440 | tf_op jit(solution)/shard_map/ppermute | solution.py:25
  85.6 18.0 %collective-permute-start.16 = (f32[2,2,256,128]{3,2,1,0:T(8,128)S(1)}, f32[2,2,256,128]{3,2,1,0:T(8,128)S(1)}, u32[]{:S(2)}, u32[]{:S(2)}) collective-permute-start(f32[2,2,256,128]{3,2,1,0:T(8,128)S(1)} %get-tuple-element.41.rest_0_.refs_1_), channel_id=1, source_target_pairs={{0,2},{1,3},{2,0},{3,1},{4,6},{5,7},{6,4},{7,5},{8,10},{9,11},{10,... | collective-permute-start | bytes 1572872 | tf_op jit(solution)/shard_map/ppermute | solution.py:25
  86.2 8.4 %collective-permute-start.7 = (f32[512,128]{1,0:T(8,128)S(1)}, f32[512,128]{1,0:T(8,128)S(1)}, u32[]{:S(2)}, u32[]{:S(2)}) collective-permute-start(f32[512,128]{1,0:T(8,128)S(1)} %get-tuple-element.38.rest_1_), channel_id=1, source_target_pairs={{0,4},{4,0},{8,12},{12,8},{16,20},{20,16},{24,28},{28,24},{1,5},{5... | collective-permute-start | bytes 786440 | tf_op jit(solution)/shard_map/ppermute | solution.py:25
  95.6 15.6 %collective-permute-start.14 = (f32[2,2,256,128]{3,2,1,0:T(8,128)S(1)}, f32[2,2,256,128]{3,2,1,0:T(8,128)S(1)}, u32[]{:S(2)}, u32[]{:S(2)}) collective-permute-start(f32[2,2,256,128]{3,2,1,0:T(8,128)S(1)} %get-tuple-element.42.refs_3_.refs_1_), channel_id=1, source_target_pairs={{0,2},{1,3},{2,0},{3,1},{4,6},{5,7},{6,4},{7,5},{8,10},{9,11},{10,... | collective-permute-start | bytes 1572872 | tf_op jit(solution)/shard_map/ppermute | solution.py:25
  97.2 7.0 %collective-permute-start.15 = (f32[2,256,128]{2,1,0:T(8,128)S(1)}, f32[2,256,128]{2,1,0:T(8,128)S(1)}, u32[]{:S(2)}, u32[]{:S(2)}) collective-permute-start(f32[2,256,128]{2,1,0:T(8,128)S(1)} %get-tuple-element.43), channel_id=1, source_target_pairs={{0,1},{1,0},{2,3},{3,2},{4,5},{5,4},{6,7},{7,6},{8,9},{9,8},{10,11... | collective-permute-start | bytes 786440 | tf_op jit(solution)/shard_map/ppermute | solution.py:25
  102.3 12.3 %collective-permute-start.13 = (f32[1024,128]{1,0:T(8,128)S(1)}, f32[1024,128]{1,0:T(8,128)S(1)}, u32[]{:S(2)}, u32[]{:S(2)}) collective-permute-start(f32[1024,128]{1,0:T(8,128)S(1)} %shard_map.60.rest_0_), channel_id=1, source_target_pairs={{0,4},{4,0},{8,12},{12,8},{16,20},{20,16},{24,28},{28,24},{1,5},{5... | collective-permute-start | bytes 1572872 | tf_op jit(solution)/shard_map/ppermute | solution.py:25
  103.7 1.6 %collective-permute-start.17 = (f32[2,256,128]{2,1,0:T(8,128)S(1)}, f32[2,256,128]{2,1,0:T(8,128)S(1)}, u32[]{:S(2)}, u32[]{:S(2)}) collective-permute-start(f32[2,256,128]{2,1,0:T(8,128)S(1)} %shard_map.61.refs_5_), channel_id=1, source_target_pairs={{0,1},{1,0},{2,3},{3,2},{4,5},{5,4},{6,7},{7,6},{8,9},{9,8},{10,11... | collective-permute-start | bytes 786440 | tf_op jit(solution)/shard_map/ppermute | solution.py:25
  103.7 15.0 %collective-permute-start.22 = (f32[1024,128]{1,0:T(8,128)S(1)}, f32[1024,128]{1,0:T(8,128)S(1)}, u32[]{:S(2)}, u32[]{:S(2)}) collective-permute-start(f32[1024,128]{1,0:T(8,128)S(1)} %shard_map.58.rest_4_.refs_1_), channel_id=1, source_target_pairs={{0,1},{1,0},{2,3},{3,2},{4,5},{5,4},{6,7},{7,6},{8,9},{9,8},{10,11... | collective-permute-start | bytes 1572872 | tf_op jit(solution)/shard_map/ppermute | solution.py:25
  104.2 11.4 %collective-permute-start.23 = (f32[2,256,128]{2,1,0:T(8,128)S(1)}, f32[2,256,128]{2,1,0:T(8,128)S(1)}, u32[]{:S(2)}, u32[]{:S(2)}) collective-permute-start(f32[2,256,128]{2,1,0:T(8,128)S(1)} %get-tuple-element.46), channel_id=1, source_target_pairs={{0,1},{1,0},{2,3},{3,2},{4,5},{5,4},{6,7},{7,6},{8,9},{9,8},{10,11... | collective-permute-start | bytes 786440 | tf_op jit(solution)/shard_map/ppermute | solution.py:25
  106.3 14.2 %collective-permute-start.21 = (f32[1024,128]{1,0:T(8,128)S(1)}, f32[1024,128]{1,0:T(8,128)S(1)}, u32[]{:S(2)}, u32[]{:S(2)}) collective-permute-start(f32[1024,128]{1,0:T(8,128)S(1)} %shard_map.62.rest_0_.refs_1_), channel_id=1, source_target_pairs={{0,1},{1,0},{2,3},{3,2},{4,5},{5,4},{6,7},{7,6},{8,9},{9,8},{10,11... | collective-permute-start | bytes 1572872 | tf_op jit(solution)/shard_map/ppermute | solution.py:25
  111.2 5.4 %collective-permute-start.24 = (f32[2,256,128]{2,1,0:T(8,128)S(1)}, f32[2,256,128]{2,1,0:T(8,128)S(1)}, u32[]{:S(2)}, u32[]{:S(2)}) collective-permute-start(f32[2,256,128]{2,1,0:T(8,128)S(1)} %shard_map.63.rest_2_), channel_id=1, source_target_pairs={{0,1},{1,0},{2,3},{3,2},{4,5},{5,4},{6,7},{7,6},{8,9},{9,8},{10,11... | collective-permute-start | bytes 786440 | tf_op jit(solution)/shard_map/ppermute | solution.py:25
  115.6 6.2 %collective-permute-start.18 = (f32[2,256,128]{2,1,0:T(8,128)S(1)}, f32[2,256,128]{2,1,0:T(8,128)S(1)}, u32[]{:S(2)}, u32[]{:S(2)}) collective-permute-start(f32[2,256,128]{2,1,0:T(8,128)S(1)} %get-tuple-element.45), channel_id=1, source_target_pairs={{0,1},{1,0},{2,3},{3,2},{4,5},{5,4},{6,7},{7,6},{8,9},{9,8},{10,11... | collective-permute-start | bytes 786440 | tf_op jit(solution)/shard_map/ppermute | solution.py:25
  115.7 3.6 %copy-start.2 = (bf16[2,8,256,256]{3,2,1,0:T(8,128)(2,1)S(1)}, bf16[2,8,256,256]{3,2,1,0:T(8,128)(2,1)}, u32[]{:S(2)}) copy-start(bf16[2,8,256,256]{3,2,1,0:T(8,128)(2,1)} %copy-done.1) | copy-start | bytes 6291460
  115.7 9.2 %collective-permute-start.19 = (f32[2,256,128]{2,1,0:T(8,128)S(1)}, f32[2,256,128]{2,1,0:T(8,128)S(1)}, u32[]{:S(2)}, u32[]{:S(2)}) collective-permute-start(f32[2,256,128]{2,1,0:T(8,128)S(1)} %get-tuple-element.44.refs_5_.refs_1_), channel_id=1, source_target_pairs={{0,2},{1,3},{2,0},{3,1},{4,6},{5,7},{6,4},{7,5},{8,10},{9,11},{10,... | collective-permute-start | bytes 786440 | tf_op jit(solution)/shard_map/ppermute | solution.py:25
  116.7 12.8 %collective-permute-start.20 = (f32[2,256,128]{2,1,0:T(8,128)S(1)}, f32[2,256,128]{2,1,0:T(8,128)S(1)}, u32[]{:S(2)}, u32[]{:S(2)}) collective-permute-start(f32[2,256,128]{2,1,0:T(8,128)S(1)} %get-tuple-element.45), channel_id=1, source_target_pairs={{0,3},{1,2},{2,1},{3,0},{4,7},{5,6},{6,5},{7,4},{8,11},{9,10},{10,... | collective-permute-start | bytes 786440 | tf_op jit(solution)/shard_map/ppermute | solution.py:25
  118.8 12.2 %collective-permute-start.26 = (f32[1024,128]{1,0:T(8,128)S(1)}, f32[1024,128]{1,0:T(8,128)S(1)}, u32[]{:S(2)}, u32[]{:S(2)}) collective-permute-start(f32[1024,128]{1,0:T(8,128)S(1)} %shard_map.65.refs_3_.refs_1_), channel_id=1, source_target_pairs={{0,1},{1,0},{2,3},{3,2},{4,5},{5,4},{6,7},{7,6},{8,9},{9,8},{10,11... | collective-permute-start | bytes 1572872 | tf_op jit(solution)/shard_map/ppermute | solution.py:25
  130.6 2.0 %collective-permute-start.25 = (f32[1024,128]{1,0:T(8,128)S(1)}, f32[1024,128]{1,0:T(8,128)S(1)}, u32[]{:S(2)}, u32[]{:S(2)}) collective-permute-start(f32[1024,128]{1,0:T(8,128)S(1)} %shard_map.68.refs_3_.refs_1_), channel_id=1, source_target_pairs={{0,1},{1,0},{2,3},{3,2},{4,5},{5,4},{6,7},{7,6},{8,9},{9,8},{10,11... | collective-permute-start | bytes 1572872 | tf_op jit(solution)/shard_map/ppermute | solution.py:25

commit v3 on v2

--- a/solution.py
+++ b/solution.py
@@ -14,7 +14,7 @@
 PAD_X = 0
 LAG = (0, 2, 2, 2)
 CORE_SPLIT = 1
-Y_CUTS = (2, 2, 2, 1)
+Y_CUTS = (1, 2, 2, 1)
 JOINT = (1, 1, 1, 0)
 STAGES = (1, 3, 4, 6)
 VMEM_LIMIT = 16 * 1024 * 1024

time: 135 us -> 135 us (level)
    ppermute x27 -> x26, starting transfers between devices: 20.3 us -> 20.1 us  [partner_2(): lax.ppermute(shard, axis, [(i, i ^ mask) for i in range(lax.axis_size(axi...]
    ppermute x27 -> x26, waiting for transfers between devices: 75.5 us -> 75.4 us  [partner_2(): lax.ppermute(shard, axis, [(i, i ^ mask) for i in range(lax.axis_size(axi...]
  transfers between devices with their start and end apart: 27 -> 26, of which waited for: 13 -> 13; matrix products, arithmetic and copies ran while one was open for 1% -> 1% of each run, Pallas kernels for 18% -> 18%
where the time goes in v3:
time: 135 us
  waiting for transfers between devices  75.4 us (56%)
  Pallas kernels  29.3 us (22%)
  starting transfers between devices  20.1 us (15%)
  local copies, waits for them, and re-layouts  9.19 us (7%)
    ppermute x26, waiting for transfers between devices, partner_2(): lax.ppermute(shard, axis, [(i, i ^ mask) for i in range(lax.axis_size(axi...  75.4 us
    pallas_call x25, Pallas kernels, run(): pl.pallas_call(kernel, out_shape=out_shape, in_specs=list(in_specs) + [AN...  29.3 us
    ppermute x26, starting transfers between devices, partner_2(): lax.ppermute(shard, axis, [(i, i ^ mask) for i in range(lax.axis_size(axi...  20.1 us
    unnamed x26, local copies, waits for them, and re-layouts  8.15 us
  transfers between devices with their start and end apart: 26, of which 13 were waited for; matrix products, arithmetic and copies ran while one was open for 1% of the time, Pallas kernels for 18%

profile of v3, /device:TPU:0, one launch (start us, length us, event | category | flops | bytes accessed | tf_op | source)
XLA Modules:
  0.0 134.6 jit_solution(8928558935161588553)
XLA Ops:
  0.0 2.7 %shard_map.46.refs_2_.refs_1_ = f32[1032,128]{1,0:T(8,128)} custom-call(s32[4]{0:T(128)} %bits_hbm.27, f32[8,128,512]{2,1,0:T(8,128)} %refs_0_.3, f32[8,8,128,256]{3,2,1,0:T(8,128)} %g_hbm.1), custom_call_target="tpu_custom_call" | custom-call | tf_op jit(solution)/shard_map/pallas_call | solution.py:327
  2.7 4.1 %collective-permute-start.1 = (f32[1032,128]{1,0:T(8,128)}, f32[1032,128]{1,0:T(8,128)}, u32[]{:S(2)}, u32[]{:S(2)}) collective-permute-start(f32[1032,128]{1,0:T(8,128)} %shard_map.46.refs_2_.refs_1_), channel_id=1, source_target_pairs={{0,16},{4,20},{8,24},{12,28},{16,0},{20,4},{24,8},{28,12},{1,17},{... | collective-permute-start | bytes 1585160 | tf_op jit(solution)/shard_map/ppermute | solution.py:25
  6.8 3.8 %shard_map.47 = (f32[1032,128]{1,0:T(8,128)}, f32[1032,128]{1,0:T(8,128)}, f32[1032,128]{1,0:T(8,128)}) custom-call(s32[4]{0:T(128)} %bits_hbm.27, f32[8,128,512]{2,1,0:T(8,128)} %refs_0_.3, f32[8,8,128,256]{3,2,1,0:T(8,128)} %g_hbm.1, f32[1032,128]{1,0:T(8,128)} %shard_map.46.refs_2_.refs_1_), custom_call_target="tpu_custom_call" | custom-call | tf_op jit(solution)/shard_map/pallas_call | solution.py:327
  10.7 3.4 %copy-done = f32[8,8,128,256]{3,2,1,0:T(8,128)S(1)} copy-done((f32[8,8,128,256]{3,2,1,0:T(8,128)S(1)}, f32[8,8,128,256]{3,2,1,0:T(8,128)}, u32[]{:S(2)}) %copy-start) | copy-done | bytes 8388632
  14.1 1.0 copy-done.8
  15.1 1.6 %shard_map.48 = (bf16[2,8,256,256]{3,2,1,0:T(8,128)(2,1)S(1)}, bf16[1,8,256,256]{3,2,1,0:T(8,128)(2,1)S(1)}, bf16[2,8,256,256]{3,2,1,0:T(8,128)(2,1)S(1)}, bf16[2,8,256,256]{3,2,1,0:T(8,128)(2,1)S(1)}) custom-call(f32[8,8,128,256]{3,2,1,0:T(8,128)S(1)} %copy-done, f32[1032,128]{1,0:T(8,128)S(1)} %copy-done.8), custom_call_target="tpu_custom_call" | custom-call | tf_op jit(solution)/shard_map/pallas_call | solution.py:327
  16.8 1.3 copy-done.1
  18.1 1.3 copy-done.3
  19.4 1.0 copy.7.relabel_ref
  20.5 1.0 copy-done.10
  22.0 20.6 %collective-permute-done.1.refs_2_.__1_ = f32[1032,128]{1,0:T(8,128)} collective-permute-done((f32[1032,128]{1,0:T(8,128)}, f32[1032,128]{1,0:T(8,128)}, u32[]{:S(2)}, u32[]{:S(2)}) %collective-permute-start.1) | collective-permute-done | bytes 528416 | tf_op jit(solution)/shard_map/ppermute | solution.py:25
  42.6 2.3 %shard_map.50.__2_.rest_0_ = f32[1024,128]{1,0:T(8,128)S(1)} custom-call(s32[4]{0:T(128)S(1)} %copy-done.11, bf16[2,8,256,256]{3,2,1,0:T(8,128)(2,1)S(1)} %get-tuple-element.28.rest_0_.refs_0_, f32[1032,128]{1,0:T(8,128)S(1)} %copy-done.5, f32[1032,128]{1,0:T(8,128)} %collective-permute-done.1.refs_2_.__1_, bf16[1024,1024]{1,0:T(8,128)(2,1)S(1)} %shard_map.49.refs_3_.chosen), custom_call_target="tpu_custom_call" | custom-call | tf_op jit(solution)/shard_map/pallas_call | solution.py:327
  44.9 1.9 %collective-permute-start.4 = (f32[1024,128]{1,0:T(8,128)S(1)}, f32[1024,128]{1,0:T(8,128)S(1)}, u32[]{:S(2)}, u32[]{:S(2)}) collective-permute-start(f32[1024,128]{1,0:T(8,128)S(1)} %shard_map.50.__2_.rest_0_), channel_id=1, source_target_pairs={{0,4},{4,0},{8,12},{12,8},{16,20},{20,16},{24,28},{28,24},{1,5},{5... | collective-permute-start | bytes 1572872 | tf_op jit(solution)/shard_map/ppermute | solution.py:25
  46.8 18.4 %collective-permute-done.__1_.refs_2_ = f32[1032,128]{1,0:T(8,128)} collective-permute-done((f32[1032,128]{1,0:T(8,128)}, f32[1032,128]{1,0:T(8,128)}, u32[]{:S(2)}, u32[]{:S(2)}) %collective-permute-start) | collective-permute-done | bytes 528416 | tf_op jit(solution)/shard_map/ppermute | solution.py:25
  65.3 2.1 %shard_map.53 = (f32[512,128]{1,0:T(8,128)S(1)}, f32[512,128]{1,0:T(8,128)S(1)}) custom-call(s32[4]{0:T(128)S(1)} %copy-done.11, bf16[2,8,256,256]{3,2,1,0:T(8,128)(2,1)S(1)} %get-tuple-element.28.rest_0_.refs_0_, f32[1032,128]{1,0:T(8,128)S(1)} %copy-done.9, f32[1032,128]{1,0:T(8,128)} %collective-permute-done.__1_.refs_2_, ...), custom_call_target="tpu_custom_call" | custom-call | tf_op jit(solution)/shard_map/pallas_call | solution.py:327
  67.4 1.0 shard_map.54
  68.4 1.9 %collective-permute-start.8 = (f32[2,2,256,128]{3,2,1,0:T(8,128)S(1)}, f32[2,2,256,128]{3,2,1,0:T(8,128)S(1)}, u32[]{:S(2)}, u32[]{:S(2)}) collective-permute-start(f32[2,2,256,128]{3,2,1,0:T(8,128)S(1)} %get-tuple-element.32.refs_3_.refs_1_), channel_id=1, source_target_pairs={{0,2},{1,3},{2,0},{3,1},{4,6},{5,7},{6,4},{7,5},{8,10},{9,11},{10,... | collective-permute-start | bytes 1572872 | tf_op jit(solution)/shard_map/ppermute | solution.py:25
  70.3 1.5 %collective-permute-start.9 = (f32[512,128]{1,0:T(8,128)S(1)}, f32[512,128]{1,0:T(8,128)S(1)}, u32[]{:S(2)}, u32[]{:S(2)}) collective-permute-start(f32[512,128]{1,0:T(8,128)S(1)} %get-tuple-element.31.rest_2_.rest_0_), channel_id=1, source_target_pairs={{0,4},{4,0},{8,12},{12,8},{16,20},{20,16},{24,28},{28,24},{1,5},{5... | collective-permute-start | bytes 786440 | tf_op jit(solution)/shard_map/ppermute | solution.py:25
  72.3 3.3 %collective-permute-done.3.refs_2_ = f32[1032,128]{1,0:T(8,128)S(1)} collective-permute-done((f32[1032,128]{1,0:T(8,128)S(1)}, f32[1032,128]{1,0:T(8,128)S(1)}, u32[]{:S(2)}, u32[]{:S(2)}) %collective-permute-start.3) | collective-permute-done | bytes 528416 | tf_op jit(solution)/shard_map/ppermute | solution.py:25
  75.6 1.0 shard_map.55
  76.7 2.4 %collective-permute-done.9.rest_2_ = f32[512,128]{1,0:T(8,128)S(1)} collective-permute-done((f32[512,128]{1,0:T(8,128)S(1)}, f32[512,128]{1,0:T(8,128)S(1)}, u32[]{:S(2)}, u32[]{:S(2)}) %collective-permute-start.9) | collective-permute-done | bytes 262176 | tf_op jit(solution)/shard_map/ppermute | solution.py:25
  79.1 1.8 %collective-permute-start.5 = (f32[512,128]{1,0:T(8,128)S(1)}, f32[512,128]{1,0:T(8,128)S(1)}, u32[]{:S(2)}, u32[]{:S(2)}) collective-permute-start(f32[512,128]{1,0:T(8,128)S(1)} %get-tuple-element.33.rest_4_.rest_0_), channel_id=1, source_target_pairs={{0,4},{4,0},{8,12},{12,8},{16,20},{20,16},{24,28},{28,24},{1,5},{5... | collective-permute-start | bytes 786440 | tf_op jit(solution)/shard_map/ppermute | solution.py:25
  80.8 3.7 %collective-permute-done.10.rest_3_ = f32[512,128]{1,0:T(8,128)S(1)} collective-permute-done((f32[512,128]{1,0:T(8,128)S(1)}, f32[512,128]{1,0:T(8,128)S(1)}, u32[]{:S(2)}, u32[]{:S(2)}) %collective-permute-start.10) | collective-permute-done | bytes 262176 | tf_op jit(solution)/shard_map/ppermute | solution.py:25
  84.5 1.0 shard_map.56
  85.6 0.5 collective-permute-start.15
  86.2 1.1 collective-permute-start.6
  87.3 1.1 shard_map.58.rest_4_.refs_1_
  88.4 6.2 %collective-permute-done.6.rest_3_ = f32[512,128]{1,0:T(8,128)S(1)} collective-permute-done((f32[512,128]{1,0:T(8,128)S(1)}, f32[512,128]{1,0:T(8,128)S(1)}, u32[]{:S(2)}, u32[]{:S(2)}) %collective-permute-start.6) | collective-permute-done | bytes 262176 | tf_op jit(solution)/shard_map/ppermute | solution.py:25
  94.6 1.0 shard_map.59
  95.6 1.6 %collective-permute-start.13 = (f32[2,2,256,128]{3,2,1,0:T(8,128)S(1)}, f32[2,2,256,128]{3,2,1,0:T(8,128)S(1)}, u32[]{:S(2)}, u32[]{:S(2)}) collective-permute-start(f32[2,2,256,128]{3,2,1,0:T(8,128)S(1)} %get-tuple-element.38.refs_3_.refs_1_), channel_id=1, source_target_pairs={{0,2},{1,3},{2,0},{3,1},{4,6},{5,7},{6,4},{7,5},{8,10},{9,11},{10,... | collective-permute-start | bytes 1572872 | tf_op jit(solution)/shard_map/ppermute | solution.py:25
  97.2 3.8 %collective-permute-done.2.refs_2_ = f32[1032,128]{1,0:T(8,128)S(1)} collective-permute-done((f32[1032,128]{1,0:T(8,128)S(1)}, f32[1032,128]{1,0:T(8,128)S(1)}, u32[]{:S(2)}, u32[]{:S(2)}) %collective-permute-start.2) | collective-permute-done | bytes 528416 | tf_op jit(solution)/shard_map/ppermute | solution.py:25
  101.1 1.2 shard_map.60.rest_0_
  102.3 1.3 collective-permute-start.12
  104.3 0.9 collective-permute-done.16.refs_4_
  105.3 1.1 shard_map.62.rest_0_.refs_1_
  106.5 4.7 %collective-permute-done.13.joint.refs_3_ = f32[2,2,256,128]{3,2,1,0:T(8,128)S(1)} collective-permute-done((f32[2,2,256,128]{3,2,1,0:T(8,128)S(1)}, f32[2,2,256,128]{3,2,1,0:T(8,128)S(1)}, u32[]{:S(2)}, u32[]{:S(2)}) %collective-permute-start.13) | collective-permute-done | bytes 524320 | tf_op jit(solution)/shard_map/ppermute | solution.py:25
  111.3 3.2 %collective-permute-done.12.rest_1_ = f32[1024,128]{1,0:T(8,128)S(1)} collective-permute-done((f32[1024,128]{1,0:T(8,128)S(1)}, f32[1024,128]{1,0:T(8,128)S(1)}, u32[]{:S(2)}, u32[]{:S(2)}) %collective-permute-start.12) | collective-permute-done | bytes 524320 | tf_op jit(solution)/shard_map/ppermute | solution.py:25
  114.6 1.0 shard_map.64
  115.7 1.0 collective-permute-start.18
  116.7 0.8 collective-permute-start.19
  117.5 1.2 shard_map.65.refs_3_.refs_1_
  119.2 1.3 shard_map.66.refs_3_
  120.5 1.3 shard_map.67.refs_5_.refs_4_
  121.8 3.1 %collective-permute-done.18.refs_3_ = f32[2,256,128]{2,1,0:T(8,128)S(1)} collective-permute-done((f32[2,256,128]{2,1,0:T(8,128)S(1)}, f32[2,256,128]{2,1,0:T(8,128)S(1)}, u32[]{:S(2)}, u32[]{:S(2)}) %collective-permute-start.18) | collective-permute-done | bytes 262176 | tf_op jit(solution)/shard_map/ppermute | solution.py:25
  124.9 4.7 %collective-permute-done.19.refs_4_ = f32[2,256,128]{2,1,0:T(8,128)S(1)} collective-permute-done((f32[2,256,128]{2,1,0:T(8,128)S(1)}, f32[2,256,128]{2,1,0:T(8,128)S(1)}, u32[]{:S(2)}, u32[]{:S(2)}) %collective-permute-start.19) | collective-permute-done | bytes 262176 | tf_op jit(solution)/shard_map/ppermute | solution.py:25
  129.5 1.1 shard_map.68.refs_3_.refs_1_
  131.0 1.3 shard_map.69.refs_5_.refs_6_
  132.6 1.8 %shard_map.70 = f32[8,128,512]{2,1,0:T(8,128)} custom-call(s32[4]{0:T(128)S(1)} %copy-done.11, bf16[2,8,256,256]{3,2,1,0:T(8,128)(2,1)S(1)} %copy-done.2, f32[1024,128]{1,0:T(8,128)S(1)} %shard_map.68.refs_3_.refs_1_, f32[1024,128]{1,0:T(8,128)S(1)} %collective-permute-done.24.refs_2_, f32[1024,128]{1,0:T(8,128)S(1)} %shard_map.66.refs_3_, ...), custom_call_target="tpu_custom_call" | custom-call | tf_op jit(solution)/shard_map/pallas_call | solution.py:327
  (56 shorter events, 3.3 us)
Async XLA Ops:
  2.7 39.9 %collective-permute-start.1 = (f32[1032,128]{1,0:T(8,128)}, f32[1032,128]{1,0:T(8,128)}, u32[]{:S(2)}, u32[]{:S(2)}) collective-permute-start(f32[1032,128]{1,0:T(8,128)} %shard_map.46.refs_2_.refs_1_), channel_id=1, source_target_pairs={{0,16},{4,20},{8,24},{12,28},{16,0},{20,4},{24,8},{28,12},{1,17},{... | collective-permute-start | bytes 1585160 | tf_op jit(solution)/shard_map/ppermute | solution.py:25
  10.6 54.6 %collective-permute-start = (f32[1032,128]{1,0:T(8,128)}, f32[1032,128]{1,0:T(8,128)}, u32[]{:S(2)}, u32[]{:S(2)}) collective-permute-start(f32[1032,128]{1,0:T(8,128)} %get-tuple-element.24.rest_0_.refs_1_), channel_id=1, source_target_pairs={{0,16},{4,20},{8,24},{12,28},{16,0},{20,4},{24,8},{28,12},{1,17},{... | collective-permute-start | bytes 1585160 | tf_op jit(solution)/shard_map/ppermute | solution.py:25
  10.7 3.4 %copy-start = (f32[8,8,128,256]{3,2,1,0:T(8,128)S(1)}, f32[8,8,128,256]{3,2,1,0:T(8,128)}, u32[]{:S(2)}) copy-start(f32[8,8,128,256]{3,2,1,0:T(8,128)} %g_hbm.1) | copy-start | bytes 25165828
  14.1 1.0 copy-start.8
  15.1 4.3 %copy-start.12 = (s32[1024]{0:T(1024)S(1)}, s32[1024]{0:T(1024)}, u32[]{:S(2)}) copy-start(s32[1024]{0:T(1024)} %param.7) | copy-start | bytes 12292
  16.8 1.3 copy-start.1
  18.1 1.3 %copy-start.3 = (bf16[2,8,256,256]{3,2,1,0:T(8,128)(2,1)}, bf16[2,8,256,256]{3,2,1,0:T(8,128)(2,1)S(1)}, u32[]{:S(2)}) copy-start(bf16[2,8,256,256]{3,2,1,0:T(8,128)(2,1)S(1)} %get-tuple-element.26.refs_0_) | copy-start | bytes 6291460
  20.5 1.0 copy-start.10
  21.5 21.1 %copy-start.5 = (f32[1032,128]{1,0:T(8,128)S(1)}, f32[1032,128]{1,0:T(8,128)}, u32[]{:S(2)}) copy-start(f32[1032,128]{1,0:T(8,128)} %shard_map.46.refs_2_.refs_1_) | copy-start | bytes 1585156
  21.5 21.1 %copy-start.11 = (s32[4]{0:T(128)S(1)}, s32[4]{0:T(128)}, u32[]{:S(2)}) copy-start(s32[4]{0:T(128)} %bits_hbm.27) | copy-start | bytes 52
  21.9 24.9 %copy-start.7 = (f32[1032,128]{1,0:T(8,128)S(1)}, f32[1032,128]{1,0:T(8,128)}, u32[]{:S(2)}) copy-start(f32[1032,128]{1,0:T(8,128)} %get-tuple-element.30.__0_) | copy-start | bytes 1585156
  44.9 20.4 %copy-start.6 = (f32[1032,128]{1,0:T(8,128)S(1)}, f32[1032,128]{1,0:T(8,128)}, u32[]{:S(2)}) copy-start(f32[1032,128]{1,0:T(8,128)} %get-tuple-element.29.__0_) | copy-start | bytes 1585156
  44.9 22.5 %collective-permute-start.4 = (f32[1024,128]{1,0:T(8,128)S(1)}, f32[1024,128]{1,0:T(8,128)S(1)}, u32[]{:S(2)}, u32[]{:S(2)}) collective-permute-start(f32[1024,128]{1,0:T(8,128)S(1)} %shard_map.50.__2_.rest_0_), channel_id=1, source_target_pairs={{0,4},{4,0},{8,12},{12,8},{16,20},{20,16},{24,28},{28,24},{1,5},{5... | collective-permute-start | bytes 1572872 | tf_op jit(solution)/shard_map/ppermute | solution.py:25
  46.8 18.4 %copy-start.9 = (f32[1032,128]{1,0:T(8,128)S(1)}, f32[1032,128]{1,0:T(8,128)}, u32[]{:S(2)}) copy-start(f32[1032,128]{1,0:T(8,128)} %get-tuple-element.24.rest_0_.refs_1_) | copy-start | bytes 1585156
  46.8 28.8 %collective-permute-start.3 = (f32[1032,128]{1,0:T(8,128)S(1)}, f32[1032,128]{1,0:T(8,128)S(1)}, u32[]{:S(2)}, u32[]{:S(2)}) collective-permute-start(f32[1032,128]{1,0:T(8,128)S(1)} %shard_map.51.__2_.refs_1_), channel_id=1, source_target_pairs={{0,16},{4,20},{8,24},{12,28},{16,0},{20,4},{24,8},{28,12},{1,17},{... | collective-permute-start | bytes 1585160 | tf_op jit(solution)/shard_map/ppermute | solution.py:25
  68.4 17.1 %collective-permute-start.8 = (f32[2,2,256,128]{3,2,1,0:T(8,128)S(1)}, f32[2,2,256,128]{3,2,1,0:T(8,128)S(1)}, u32[]{:S(2)}, u32[]{:S(2)}) collective-permute-start(f32[2,2,256,128]{3,2,1,0:T(8,128)S(1)} %get-tuple-element.32.refs_3_.refs_1_), channel_id=1, source_target_pairs={{0,2},{1,3},{2,0},{3,1},{4,6},{5,7},{6,4},{7,5},{8,10},{9,11},{10,... | collective-permute-start | bytes 1572872 | tf_op jit(solution)/shard_map/ppermute | solution.py:25
  70.3 8.8 %collective-permute-start.9 = (f32[512,128]{1,0:T(8,128)S(1)}, f32[512,128]{1,0:T(8,128)S(1)}, u32[]{:S(2)}, u32[]{:S(2)}) collective-permute-start(f32[512,128]{1,0:T(8,128)S(1)} %get-tuple-element.31.rest_2_.rest_0_), channel_id=1, source_target_pairs={{0,4},{4,0},{8,12},{12,8},{16,20},{20,16},{24,28},{28,24},{1,5},{5... | collective-permute-start | bytes 786440 | tf_op jit(solution)/shard_map/ppermute | solution.py:25
  71.8 12.7 %collective-permute-start.10 = (f32[512,128]{1,0:T(8,128)S(1)}, f32[512,128]{1,0:T(8,128)S(1)}, u32[]{:S(2)}, u32[]{:S(2)}) collective-permute-start(f32[512,128]{1,0:T(8,128)S(1)} %get-tuple-element.36.rest_1_), channel_id=1, source_target_pairs={{0,4},{4,0},{8,12},{12,8},{16,20},{20,16},{24,28},{28,24},{1,5},{5... | collective-permute-start | bytes 786440 | tf_op jit(solution)/shard_map/ppermute | solution.py:25
  72.3 13.9 %collective-permute-start.7 = (f32[2,256,128]{2,1,0:T(8,128)S(1)}, f32[2,256,128]{2,1,0:T(8,128)S(1)}, u32[]{:S(2)}, u32[]{:S(2)}) collective-permute-start(f32[2,256,128]{2,1,0:T(8,128)S(1)} %get-tuple-element.35), channel_id=1, source_target_pairs={{0,1},{1,0},{2,3},{3,2},{4,5},{5,4},{6,7},{7,6},{8,9},{9,8},{10,11... | collective-permute-start | bytes 786440 | tf_op jit(solution)/shard_map/ppermute | solution.py:25
  75.6 25.4 %collective-permute-start.2 = (f32[1032,128]{1,0:T(8,128)S(1)}, f32[1032,128]{1,0:T(8,128)S(1)}, u32[]{:S(2)}, u32[]{:S(2)}) collective-permute-start(f32[1032,128]{1,0:T(8,128)S(1)} %shard_map.52.refs_3_.refs_1_), channel_id=1, source_target_pairs={{0,16},{4,20},{8,24},{12,28},{16,0},{20,4},{24,8},{28,12},{1,17},{... | collective-permute-start | bytes 1585160 | tf_op jit(solution)/shard_map/ppermute | solution.py:25
  79.1 8.3 %copy-start.4 = (bf16[2,8,256,256]{3,2,1,0:T(8,128)(2,1)S(1)}, bf16[2,8,256,256]{3,2,1,0:T(8,128)(2,1)}, u32[]{:S(2)}) copy-start(bf16[2,8,256,256]{3,2,1,0:T(8,128)(2,1)} %copy-done.3) | copy-start | bytes 6291460
  79.1 9.3 %collective-permute-start.5 = (f32[512,128]{1,0:T(8,128)S(1)}, f32[512,128]{1,0:T(8,128)S(1)}, u32[]{:S(2)}, u32[]{:S(2)}) collective-permute-start(f32[512,128]{1,0:T(8,128)S(1)} %get-tuple-element.33.rest_4_.rest_0_), channel_id=1, source_target_pairs={{0,4},{4,0},{8,12},{12,8},{16,20},{20,16},{24,28},{28,24},{1,5},{5... | collective-permute-start | bytes 786440 | tf_op jit(solution)/shard_map/ppermute | solution.py:25
  85.6 1.8 %collective-permute-start.11 = (f32[2,256,128]{2,1,0:T(8,128)S(1)}, f32[2,256,128]{2,1,0:T(8,128)S(1)}, u32[]{:S(2)}, u32[]{:S(2)}) collective-permute-start(f32[2,256,128]{2,1,0:T(8,128)S(1)} %shard_map.57.refs_5_), channel_id=1, source_target_pairs={{0,1},{1,0},{2,3},{3,2},{4,5},{5,4},{6,7},{7,6},{8,9},{9,8},{10,11... | collective-permute-start | bytes 786440 | tf_op jit(solution)/shard_map/ppermute | solution.py:25
  85.6 18.0 %collective-permute-start.15 = (f32[2,2,256,128]{3,2,1,0:T(8,128)S(1)}, f32[2,2,256,128]{3,2,1,0:T(8,128)S(1)}, u32[]{:S(2)}, u32[]{:S(2)}) collective-permute-start(f32[2,2,256,128]{3,2,1,0:T(8,128)S(1)} %get-tuple-element.37.rest_0_.refs_1_), channel_id=1, source_target_pairs={{0,2},{1,3},{2,0},{3,1},{4,6},{5,7},{6,4},{7,5},{8,10},{9,11},{10,... | collective-permute-start | bytes 1572872 | tf_op jit(solution)/shard_map/ppermute | solution.py:25
  86.2 8.4 %collective-permute-start.6 = (f32[512,128]{1,0:T(8,128)S(1)}, f32[512,128]{1,0:T(8,128)S(1)}, u32[]{:S(2)}, u32[]{:S(2)}) collective-permute-start(f32[512,128]{1,0:T(8,128)S(1)} %get-tuple-element.34.rest_1_), channel_id=1, source_target_pairs={{0,4},{4,0},{8,12},{12,8},{16,20},{20,16},{24,28},{28,24},{1,5},{5... | collective-permute-start | bytes 786440 | tf_op jit(solution)/shard_map/ppermute | solution.py:25
  95.6 15.6 %collective-permute-start.13 = (f32[2,2,256,128]{3,2,1,0:T(8,128)S(1)}, f32[2,2,256,128]{3,2,1,0:T(8,128)S(1)}, u32[]{:S(2)}, u32[]{:S(2)}) collective-permute-start(f32[2,2,256,128]{3,2,1,0:T(8,128)S(1)} %get-tuple-element.38.refs_3_.refs_1_), channel_id=1, source_target_pairs={{0,2},{1,3},{2,0},{3,1},{4,6},{5,7},{6,4},{7,5},{8,10},{9,11},{10,... | collective-permute-start | bytes 1572872 | tf_op jit(solution)/shard_map/ppermute | solution.py:25
  97.2 7.0 %collective-permute-start.14 = (f32[2,256,128]{2,1,0:T(8,128)S(1)}, f32[2,256,128]{2,1,0:T(8,128)S(1)}, u32[]{:S(2)}, u32[]{:S(2)}) collective-permute-start(f32[2,256,128]{2,1,0:T(8,128)S(1)} %get-tuple-element.39), channel_id=1, source_target_pairs={{0,1},{1,0},{2,3},{3,2},{4,5},{5,4},{6,7},{7,6},{8,9},{9,8},{10,11... | collective-permute-start | bytes 786440 | tf_op jit(solution)/shard_map/ppermute | solution.py:25
  102.3 12.3 %collective-permute-start.12 = (f32[1024,128]{1,0:T(8,128)S(1)}, f32[1024,128]{1,0:T(8,128)S(1)}, u32[]{:S(2)}, u32[]{:S(2)}) collective-permute-start(f32[1024,128]{1,0:T(8,128)S(1)} %shard_map.60.rest_0_), channel_id=1, source_target_pairs={{0,4},{4,0},{8,12},{12,8},{16,20},{20,16},{24,28},{28,24},{1,5},{5... | collective-permute-start | bytes 1572872 | tf_op jit(solution)/shard_map/ppermute | solution.py:25
  103.7 1.6 %collective-permute-start.16 = (f32[2,256,128]{2,1,0:T(8,128)S(1)}, f32[2,256,128]{2,1,0:T(8,128)S(1)}, u32[]{:S(2)}, u32[]{:S(2)}) collective-permute-start(f32[2,256,128]{2,1,0:T(8,128)S(1)} %shard_map.61.refs_5_), channel_id=1, source_target_pairs={{0,1},{1,0},{2,3},{3,2},{4,5},{5,4},{6,7},{7,6},{8,9},{9,8},{10,11... | collective-permute-start | bytes 786440 | tf_op jit(solution)/shard_map/ppermute | solution.py:25
  103.7 15.1 %collective-permute-start.21 = (f32[1024,128]{1,0:T(8,128)S(1)}, f32[1024,128]{1,0:T(8,128)S(1)}, u32[]{:S(2)}, u32[]{:S(2)}) collective-permute-start(f32[1024,128]{1,0:T(8,128)S(1)} %shard_map.58.rest_4_.refs_1_), channel_id=1, source_target_pairs={{0,1},{1,0},{2,3},{3,2},{4,5},{5,4},{6,7},{7,6},{8,9},{9,8},{10,11... | collective-permute-start | bytes 1572872 | tf_op jit(solution)/shard_map/ppermute | solution.py:25
  104.2 11.4 %collective-permute-start.22 = (f32[2,256,128]{2,1,0:T(8,128)S(1)}, f32[2,256,128]{2,1,0:T(8,128)S(1)}, u32[]{:S(2)}, u32[]{:S(2)}) collective-permute-start(f32[2,256,128]{2,1,0:T(8,128)S(1)} %get-tuple-element.42), channel_id=1, source_target_pairs={{0,1},{1,0},{2,3},{3,2},{4,5},{5,4},{6,7},{7,6},{8,9},{9,8},{10,11... | collective-permute-start | bytes 786440 | tf_op jit(solution)/shard_map/ppermute | solution.py:25
  106.3 14.2 %collective-permute-start.20 = (f32[1024,128]{1,0:T(8,128)S(1)}, f32[1024,128]{1,0:T(8,128)S(1)}, u32[]{:S(2)}, u32[]{:S(2)}) collective-permute-start(f32[1024,128]{1,0:T(8,128)S(1)} %shard_map.62.rest_0_.refs_1_), channel_id=1, source_target_pairs={{0,1},{1,0},{2,3},{3,2},{4,5},{5,4},{6,7},{7,6},{8,9},{9,8},{10,11... | collective-permute-start | bytes 1572872 | tf_op jit(solution)/shard_map/ppermute | solution.py:25
  111.2 5.5 %collective-permute-start.23 = (f32[2,256,128]{2,1,0:T(8,128)S(1)}, f32[2,256,128]{2,1,0:T(8,128)S(1)}, u32[]{:S(2)}, u32[]{:S(2)}) collective-permute-start(f32[2,256,128]{2,1,0:T(8,128)S(1)} %shard_map.63.rest_2_), channel_id=1, source_target_pairs={{0,1},{1,0},{2,3},{3,2},{4,5},{5,4},{6,7},{7,6},{8,9},{9,8},{10,11... | collective-permute-start | bytes 786440 | tf_op jit(solution)/shard_map/ppermute | solution.py:25
  115.6 6.2 %collective-permute-start.17 = (f32[2,256,128]{2,1,0:T(8,128)S(1)}, f32[2,256,128]{2,1,0:T(8,128)S(1)}, u32[]{:S(2)}, u32[]{:S(2)}) collective-permute-start(f32[2,256,128]{2,1,0:T(8,128)S(1)} %get-tuple-element.41), channel_id=1, source_target_pairs={{0,1},{1,0},{2,3},{3,2},{4,5},{5,4},{6,7},{7,6},{8,9},{9,8},{10,11... | collective-permute-start | bytes 786440 | tf_op jit(solution)/shard_map/ppermute | solution.py:25
  115.7 3.6 %copy-start.2 = (bf16[2,8,256,256]{3,2,1,0:T(8,128)(2,1)S(1)}, bf16[2,8,256,256]{3,2,1,0:T(8,128)(2,1)}, u32[]{:S(2)}) copy-start(bf16[2,8,256,256]{3,2,1,0:T(8,128)(2,1)} %copy-done.1) | copy-start | bytes 6291460
  115.7 9.2 %collective-permute-start.18 = (f32[2,256,128]{2,1,0:T(8,128)S(1)}, f32[2,256,128]{2,1,0:T(8,128)S(1)}, u32[]{:S(2)}, u32[]{:S(2)}) collective-permute-start(f32[2,256,128]{2,1,0:T(8,128)S(1)} %get-tuple-element.40.refs_5_.refs_1_), channel_id=1, source_target_pairs={{0,2},{1,3},{2,0},{3,1},{4,6},{5,7},{6,4},{7,5},{8,10},{9,11},{10,... | collective-permute-start | bytes 786440 | tf_op jit(solution)/shard_map/ppermute | solution.py:25
  116.7 12.8 %collective-permute-start.19 = (f32[2,256,128]{2,1,0:T(8,128)S(1)}, f32[2,256,128]{2,1,0:T(8,128)S(1)}, u32[]{:S(2)}, u32[]{:S(2)}) collective-permute-start(f32[2,256,128]{2,1,0:T(8,128)S(1)} %get-tuple-element.41), channel_id=1, source_target_pairs={{0,3},{1,2},{2,1},{3,0},{4,7},{5,6},{6,5},{7,4},{8,11},{9,10},{10,... | collective-permute-start | bytes 786440 | tf_op jit(solution)/shard_map/ppermute | solution.py:25
  118.8 12.2 %collective-permute-start.25 = (f32[1024,128]{1,0:T(8,128)S(1)}, f32[1024,128]{1,0:T(8,128)S(1)}, u32[]{:S(2)}, u32[]{:S(2)}) collective-permute-start(f32[1024,128]{1,0:T(8,128)S(1)} %shard_map.65.refs_3_.refs_1_), channel_id=1, source_target_pairs={{0,1},{1,0},{2,3},{3,2},{4,5},{5,4},{6,7},{7,6},{8,9},{9,8},{10,11... | collective-permute-start | bytes 1572872 | tf_op jit(solution)/shard_map/ppermute | solution.py:25
  130.6 2.0 %collective-permute-start.24 = (f32[1024,128]{1,0:T(8,128)S(1)}, f32[1024,128]{1,0:T(8,128)S(1)}, u32[]{:S(2)}, u32[]{:S(2)}) collective-permute-start(f32[1024,128]{1,0:T(8,128)S(1)} %shard_map.68.refs_3_.refs_1_), channel_id=1, source_target_pairs={{0,1},{1,0},{2,3},{3,2},{4,5},{5,4},{6,7},{7,6},{8,9},{9,8},{10,11... | collective-permute-start | bytes 1572872 | tf_op jit(solution)/shard_map/ppermute | solution.py:25
